TPU v7x, 256 devices: a whole 4x4x8 slice. The times are simulated.
256 devices in a mesh: gx: 32 (over z, x), gy: 8 (over y, core).
Axes of the slice: x: 4, y: 4, z: 8, core: 2. Of those that a mesh axis runs over, the one named last changes fastest.
Arguments:
- start_field: float32 [16, 512, 128, 128], P(None, 'gx', 'gy'), may hold values from -4 to 4
- currents: float32 [256, 16], replicated, may hold values from -6 to 6
- electrode_map: int32 [2, 512, 128], P(None, 'gx', 'gy'), may hold values from 0 to 256, as said below
- contact_gain: float32 [256], replicated, may hold values from 0.5 to 5
- region_label: int32 [512, 128, 128], P('gx', 'gy'), may hold values from 0 to 7
- region_cond: float32 [8], replicated, may hold values from 0.2 to 5
- texture: float32 [512, 128, 128], P('gx', 'gy'), may hold values from 0.5 to 2
Outputs:
- solution_field: float32 [16, 512, 128, 128], P(None, 'gx', 'gy')
- voltages: float32 [16, 256], replicated
Inputs may be any that keep to these rules, and one draw needn't show every extreme that they name: `electrode_map`: each of the 256 electrode numbers 1 to 256 covers exactly one square of 2 x 2 voxels aligned to multiples of 2 on one of the two end faces; all other voxels hold 0.
All inputs are finite; a program needn't handle non-finite values.
Results may differ from a plain program's by a relative error of at most 0.0003.
Values sent between devices are 32-bit elements; how exact they have to be, the bound alone decides.
No kernel may reach another device: no remote copies, remote signals or barrier semaphores. Data moves between devices by JAX's collectives and lax.ppermute only.
A program may use at most 128 MiB of HBM per device.

v0:
```python
import jax
import jax.numpy as jnp
from jax import lax
from jax.sharding import PartitionSpec as P

ELECTRODES = 256
REGIONS = 8
PATCH = 2
SWEEPS = 3
ITERS = 2


CHEB_LOW = 0.1
CHEB_HIGH = 2.0


def padded_2(shard, sides, width):
    for axis, dim in sides:
        count, length = (lax.axis_size(axis), shard.shape[dim])
        up = [(i, (i + 1) % count) for i in range(count - 1)]
        down = [(j, i) for i, j in up]
        last = lax.slice_in_dim(shard, length - width, length, axis=dim)
        initial = lax.slice_in_dim(shard, 0, width, axis=dim)
        before = lax.ppermute(last, axis, up)
        after = lax.ppermute(initial, axis, down)
        shard = jnp.concatenate([before, shard, after], axis=dim)
    return shard


def harmonic(own_cond, nbr_cond):
    summed = own_cond + nbr_cond
    divisor = jnp.where(summed > 0, summed, 1.0)
    return 2.0 * own_cond * nbr_cond / divisor


def electrode_onehot(electrode_map):
    numbers = jnp.arange(1, ELECTRODES + 1, dtype=jnp.int32)
    return (electrode_map[..., None] == numbers).astype(jnp.float32)


def region_conductivity(region_label, region_cond, texture):
    numbers = jnp.arange(REGIONS, dtype=jnp.int32)
    onehot = (region_label[..., None] == numbers).astype(jnp.float32)
    return jnp.sum(onehot * region_cond, axis=-1) * texture


def place_ends(lower_face, upper_face, z_cells):
    zindex = lax.broadcasted_iota(jnp.int32, lower_face.shape + (z_cells,), lower_face.ndim)
    return jnp.where(zindex == 0, lower_face[..., None], 0.0) + jnp.where(
        zindex == z_cells - 1, upper_face[..., None], 0.0
    )


def coefficients(widened, contact_diag):
    centre = widened[1:-1, 1:-1]
    deep_pad = jnp.pad(centre, ((0, 0), (0, 0), (1, 1)))
    lower_x = harmonic(centre, widened[:-2, 1:-1])
    upper_x = harmonic(centre, widened[2:, 1:-1])
    lower_y = harmonic(centre, widened[1:-1, :-2])
    upper_y = harmonic(centre, widened[1:-1, 2:])
    lower_z = harmonic(centre, deep_pad[:, :, :-2])
    upper_z = harmonic(centre, deep_pad[:, :, 2:])
    diagonal = contact_diag + lower_x + upper_x + lower_y + upper_y + lower_z + upper_z
    positive = diagonal > 0
    inverse = jnp.where(positive, 1.0 / jnp.where(positive, diagonal, 1.0), 0.0)
    return ((lower_x, upper_x, lower_y, upper_y, lower_z, upper_z, contact_diag), inverse)


def stencil(padded, couplings):
    lower_x, upper_x, lower_y, upper_y, lower_z, upper_z, contact_diag = couplings
    centre = padded[:, 1:-1, 1:-1]
    deep_pad = jnp.pad(centre, ((0, 0), (0, 0), (0, 0), (1, 1)))
    return (
        contact_diag * centre
        + lower_x * (centre - padded[:, :-2, 1:-1])
        + upper_x * (centre - padded[:, 2:, 1:-1])
        + lower_y * (centre - padded[:, 1:-1, :-2])
        + upper_y * (centre - padded[:, 1:-1, 2:])
        + lower_z * (centre - deep_pad[..., :-2])
        + upper_z * (centre - deep_pad[..., 2:])
    )


def chebyshev(residual, operate_fn, inverse):
    middle = 0.5 * (CHEB_HIGH + CHEB_LOW)
    radius = 0.5 * (CHEB_HIGH - CHEB_LOW)
    sharpness = middle / radius
    rho_now = 1.0 / sharpness
    update = inverse * residual / middle
    iterate = update
    for sweep_index in range(SWEEPS):
        defect = inverse * (residual - operate_fn(iterate))
        rho_next = 1.0 / (2.0 * sharpness - rho_now)
        update = rho_next * rho_now * update + 2.0 * rho_next / radius * defect
        iterate = iterate + update
        rho_now = rho_next
    return iterate


def gram_matrix(first_set, second_set):
    return jnp.einsum("pxyz,qxyz->pq", first_set, second_set, precision=lax.Precision.HIGHEST)


def combine(vectors, mixing):
    return jnp.einsum("pxyz,pq->qxyz", vectors, mixing, precision=lax.Precision.HIGHEST)


def direction_apply(values, couplings):
    padded = padded_2(values, (("gx", 1), ("gy", 2)), 1)
    return stencil(padded, couplings)


def body(start_field, currents, electrode_map, contact_gain, region_label, region_cond, texture):
    z_cells = texture.shape[2]
    onehot_faces = electrode_onehot(electrode_map)
    contact_faces = jnp.einsum(
        "fxye,e->fxy", onehot_faces, contact_gain, precision=lax.Precision.HIGHEST
    )
    contact_diag = place_ends(contact_faces[0], contact_faces[1], z_cells)
    source_faces = jnp.einsum(
        "fxye,ep->pfxy", onehot_faces, currents, precision=lax.Precision.HIGHEST
    )
    source = place_ends(source_faces[:, 0], source_faces[:, 1], z_cells)
    conduct = region_conductivity(region_label, region_cond, texture)
    widened = padded_2(conduct, (("gx", 0), ("gy", 1)), 1)
    couplings, local_inverse = coefficients(widened, contact_diag)

    def sweep_apply(values):
        padded = padded_2(values, (("gx", 1), ("gy", 2)), 1)
        return stencil(padded, couplings)

    solution = start_field
    residual = source - direction_apply(start_field, couplings)
    direction = residual
    mapped = residual
    factor = jnp.eye(start_field.shape[0], dtype=jnp.float32)
    for iter_index in range(ITERS):
        smoothed = chebyshev(residual, sweep_apply, local_inverse)
        if iter_index == 0:
            direction = smoothed
        else:
            cross_terms = lax.psum(gram_matrix(mapped, smoothed), ("gx", "gy"))
            beta_coef = -jax.scipy.linalg.cho_solve((factor, True), cross_terms)
            direction = smoothed + combine(direction, beta_coef)
        mapped = direction_apply(direction, couplings)
        curvature, projected = lax.psum(
            (gram_matrix(direction, mapped), gram_matrix(direction, residual)), ("gx", "gy")
        )
        curvature = 0.5 * (curvature + curvature.T)
        factor = jnp.linalg.cholesky(curvature)
        alpha_coef = jax.scipy.linalg.cho_solve((factor, True), projected)
        solution = solution + combine(direction, alpha_coef)
        if iter_index + 1 < ITERS:
            residual = residual - combine(mapped, alpha_coef)
    surface = jnp.stack((solution[..., 0], solution[..., z_cells - 1]), axis=1)
    voltages = lax.psum(
        jnp.einsum("fxye,pfxy->pe", onehot_faces, surface, precision=lax.Precision.HIGHEST),
        ("gx", "gy"),
    )
    return (solution, voltages / (PATCH * PATCH))


def solution(mesh):
    placed = (
        P(None, "gx", "gy", None),
        P(),
        P(None, "gx", "gy"),
        P(),
        P("gx", "gy", None),
        P(),
        P("gx", "gy", None),
    )
    return jax.shard_map(
        body,
        mesh=mesh,
        in_specs=placed,
        out_specs=(P(None, "gx", "gy", None), P()),
        check_vma=False,
    )
```

profile of v0, /device:TPU:1, one launch (start us, length us, event | category | flops | bytes accessed | tf_op | source)
XLA Modules:
  0.0 593.8 jit_solution(16925351712145003027)
XLA Ops:
  2.9 3.9 collective-permute-start
  11.2 4.0 collective-permute-start.4
  18.1 4.6 collective-permute-start.2
  31.9 4.2 collective-permute-done.7
  36.1 3.8 multiply_multiply_fusion.1
  40.0 4.3 collective-permute-start.8
  50.0 4.1 collective-permute-start.10
  56.2 4.4 collective-permute-done.11
  63.7 3.9 collective-permute-start.12
  69.6 6.2 %collective-permute-done.13 = f32[16,1,16,128]{3,0,2,1:T(8,128)S(1)} collective-permute-done((f32[16,1,16,128]{3,0,2,1:T(8,128)S(1)}, f32[16,1,16,128]{3,0,2,1:T(8,128)S(1)}, u32[]{:S(2)}, u32[]{:S(2)}) %collective-permute-start.13) | collective-permute-done | bytes 131104 | tf_op jit(solution)/shard_map/ppermute | solution.py:25
  81.0 4.4 collective-permute-done.15
  88.7 6.2 %collective-permute-start.16 = (f32[16,1,16,128]{3,0,2,1:T(8,128)S(1)}, f32[16,1,16,128]{3,0,2,1:T(8,128)S(1)}, u32[]{:S(2)}, u32[]{:S(2)}) collective-permute-start(f32[16,1,16,128]{3,0,2,1:T(8,128)S(1)} %get-tuple-element.63), channel_id=1, source_target_pairs={{0,8},{8,16},{16,24},{24,32},{32,40},{40,48},{48,56},{56,64},{64,7... | collective-permute-start | bytes 393224 | tf_op jit(solution)/shard_map/ppermute | solution.py:24
  96.8 4.4 collective-permute-done.17
  106.5 4.4 collective-permute-done.19
  119.6 3.9 collective-permute-done.21
  136.6 4.3 convolution_bitcast_fusion.7
  140.9 88.5 %all-reduce.11 = (f32[16,16]{1,0:T(8,128)S(1)}, f32[16,16]{1,0:T(8,128)S(1)}) all-reduce(f32[16,16]{1,0:T(8,128)S(1)} %convolution_bitcast_fusion.6, f32[16,16]{1,0:T(8,128)S(1)} %convolution_bitcast_fusion.7), channel_id=1, replica_groups=mesh['gx'=32,'gy'=8] {'gx','gy'}, use_global_device_ids=true, to_apply=%region_4.6 | all-reduce | flops 512 | bytes 4096 | tf_op jit(solution)/shard_map/psum | solution.py:146
  234.0 4.2 multiply_multiply_fusion
  245.3 4.4 collective-permute-start.26
  251.9 4.4 collective-permute-done.27
  264.3 4.1 collective-permute-done.29
  268.3 4.2 collective-permute-start.30
  274.6 4.4 collective-permute-done.31
  291.7 4.6 collective-permute-start.34
  298.4 4.3 collective-permute-done.35
  307.4 4.3 convolution_bitcast_fusion.4
  311.7 82.2 %psum.44 = f32[16,16]{1,0:T(8,128)S(1)} all-reduce(f32[16,16]{1,0:T(8,128)S(1)} %convolution_bitcast_fusion.4), channel_id=1, replica_groups=mesh['gx'=32,'gy'=8] {'gx','gy'}, use_global_device_ids=true, to_apply=%region_5.8 | all-reduce | flops 256 | bytes 2048 | tf_op jit(solution)/shard_map/psum | solution.py:142
  404.9 4.4 collective-permute-start.38
  415.8 4.0 fusion.201
  419.8 79.5 %all-reduce.10 = (f32[16,16]{1,0:T(8,128)S(1)}, f32[16,16]{1,0:T(8,128)S(1)}) all-reduce(f32[16,16]{1,0:T(8,128)S(1)} %convolution_bitcast_fusion.3, f32[16,16]{1,0:T(8,128)S(1)} %fusion.201), channel_id=1, replica_groups=mesh['gx'=32,'gy'=8] {'gx','gy'}, use_global_device_ids=true, to_apply=%region_7.10 | all-reduce | flops 512 | bytes 4096 | tf_op jit(solution)/shard_map/psum | solution.py:146
  503.9 5.8 add_add_fusion
  520.0 72.7 %psum.47 = f32[16,256]{1,0:T(8,128)S(1)} all-reduce(f32[16,256]{1,0:T(8,128)S(1)} %convolution_bitcast_fusion.1), channel_id=1, replica_groups=mesh['gx'=32,'gy'=8] {'gx','gy'}, use_global_device_ids=true, to_apply=%region_8.11 | all-reduce | flops 4096 | bytes 32768 | tf_op jit(solution)/shard_map/psum | solution.py:156
  (154 shorter events, 145.0 us)
Async XLA Ops:
  2.9 15.2 %collective-permute-start = (f32[1,16,128]{2,1,0:T(8,128)S(1)}, f32[1,16,128]{2,1,0:T(8,128)S(1)}, u32[]{:S(2)}, u32[]{:S(2)}) collective-permute-start(f32[1,16,128]{2,1,0:T(8,128)S(1)} %get-tuple-element.76), channel_id=1, source_target_pairs={{0,8},{8,16},{16,24},{24,32},{32,40},{40,48},{48,56},{56,64},{64,7... | collective-permute-start | bytes 24584 | tf_op jit(solution)/shard_map/ppermute | solution.py:24
  6.9 11.2 %collective-permute-start.1 = (f32[1,16,128]{2,1,0:T(8,128)S(1)}, f32[1,16,128]{2,1,0:T(8,128)S(1)}, u32[]{:S(2)}, u32[]{:S(2)}) collective-permute-start(f32[1,16,128]{2,1,0:T(8,128)S(1)} %get-tuple-element.75), channel_id=1, source_target_pairs={{8,0},{16,8},{24,16},{32,24},{40,32},{48,40},{56,48},{64,56},{72,6... | collective-permute-start | bytes 24584 | tf_op jit(solution)/shard_map/ppermute | solution.py:25
  11.2 13.5 %collective-permute-start.4 = (f32[16,1,16,128]{3,0,2,1:T(8,128)S(1)}, f32[16,1,16,128]{3,0,2,1:T(8,128)S(1)}, u32[]{:S(2)}, u32[]{:S(2)}) collective-permute-start(f32[16,1,16,128]{3,0,2,1:T(8,128)S(1)} %get-tuple-element.70), channel_id=1, source_target_pairs={{0,8},{8,16},{16,24},{24,32},{32,40},{40,48},{48,56},{56,64},{64,7... | collective-permute-start | bytes 393224 | tf_op jit(solution)/shard_map/ppermute | solution.py:24
  15.2 10.8 %collective-permute-start.5 = (f32[16,1,16,128]{3,0,2,1:T(8,128)S(1)}, f32[16,1,16,128]{3,0,2,1:T(8,128)S(1)}, u32[]{:S(2)}, u32[]{:S(2)}) collective-permute-start(f32[16,1,16,128]{3,0,2,1:T(8,128)S(1)} %get-tuple-element.69), channel_id=1, source_target_pairs={{8,0},{16,8},{24,16},{32,24},{40,32},{48,40},{56,48},{64,56},{72,6... | collective-permute-start | bytes 393224 | tf_op jit(solution)/shard_map/ppermute | solution.py:25
  18.1 13.4 %collective-permute-start.2 = (f32[18,1,128]{2,1,0:T(1,128)S(1)}, f32[18,1,128]{2,1,0:T(1,128)S(1)}, u32[]{:S(2)}, u32[]{:S(2)}) collective-permute-start(f32[18,1,128]{2,1,0:T(1,128)S(1)} %get-tuple-element.74), channel_id=1, source_target_pairs={{0,1},{1,2},{2,3},{3,4},{4,5},{5,6},{6,7},{8,9},{9,10},{10,11},{11... | collective-permute-start | bytes 27656 | tf_op jit(solution)/shard_map/ppermute | solution.py:24
  22.7 8.8 %collective-permute-start.3 = (f32[18,1,128]{2,1,0:T(1,128)S(1)}, f32[18,1,128]{2,1,0:T(1,128)S(1)}, u32[]{:S(2)}, u32[]{:S(2)}) collective-permute-start(f32[18,1,128]{2,1,0:T(1,128)S(1)} %get-tuple-element.73), channel_id=1, source_target_pairs={{1,0},{2,1},{3,2},{4,3},{5,4},{6,5},{7,6},{9,8},{10,9},{11,10},{12... | collective-permute-start | bytes 27656 | tf_op jit(solution)/shard_map/ppermute | solution.py:25
  26.0 5.9 collective-permute-start.6
  29.6 6.5 %collective-permute-start.7 = (f32[16,18,1,128]{3,0,2,1:T(8,128)S(1)}, f32[16,18,1,128]{3,0,2,1:T(8,128)S(1)}, u32[]{:S(2)}, u32[]{:S(2)}) collective-permute-start(f32[16,18,1,128]{3,0,2,1:T(8,128)S(1)} %get-tuple-element.50), channel_id=1, source_target_pairs={{1,0},{2,1},{3,2},{4,3},{5,4},{6,5},{7,6},{9,8},{10,9},{11,10},{12... | collective-permute-start | bytes 442376 | tf_op jit(solution)/shard_map/ppermute | solution.py:25
  40.0 6.2 %collective-permute-start.8 = (f32[16,1,16,128]{3,0,2,1:T(8,128)S(1)}, f32[16,1,16,128]{3,0,2,1:T(8,128)S(1)}, u32[]{:S(2)}, u32[]{:S(2)}) collective-permute-start(f32[16,1,16,128]{3,0,2,1:T(8,128)S(1)} %get-tuple-element.67), channel_id=1, source_target_pairs={{0,8},{8,16},{16,24},{24,32},{32,40},{40,48},{48,56},{56,64},{64,7... | collective-permute-start | bytes 393224 | tf_op jit(solution)/shard_map/ppermute | solution.py:24
  50.0 6.2 %collective-permute-start.10 = (f32[16,18,1,128]{3,0,2,1:T(8,128)S(1)}, f32[16,18,1,128]{3,0,2,1:T(8,128)S(1)}, u32[]{:S(2)}, u32[]{:S(2)}) collective-permute-start(f32[16,18,1,128]{3,0,2,1:T(8,128)S(1)} %get-tuple-element.47), channel_id=1, source_target_pairs={{0,1},{1,2},{2,3},{3,4},{4,5},{5,6},{6,7},{8,9},{9,10},{10,11},{11... | collective-permute-start | bytes 442376 | tf_op jit(solution)/shard_map/ppermute | solution.py:24
  54.1 6.5 %collective-permute-start.11 = (f32[16,18,1,128]{3,0,2,1:T(8,128)S(1)}, f32[16,18,1,128]{3,0,2,1:T(8,128)S(1)}, u32[]{:S(2)}, u32[]{:S(2)}) collective-permute-start(f32[16,18,1,128]{3,0,2,1:T(8,128)S(1)} %get-tuple-element.48), channel_id=1, source_target_pairs={{1,0},{2,1},{3,2},{4,3},{5,4},{6,5},{7,6},{9,8},{10,9},{11,10},{12... | collective-permute-start | bytes 442376 | tf_op jit(solution)/shard_map/ppermute | solution.py:25
  63.7 5.8 collective-permute-start.12
  67.7 8.1 %collective-permute-start.13 = (f32[16,1,16,128]{3,0,2,1:T(8,128)S(1)}, f32[16,1,16,128]{3,0,2,1:T(8,128)S(1)}, u32[]{:S(2)}, u32[]{:S(2)}) collective-permute-start(f32[16,1,16,128]{3,0,2,1:T(8,128)S(1)} %get-tuple-element.66), channel_id=1, source_target_pairs={{8,0},{16,8},{24,16},{32,24},{40,32},{48,40},{56,48},{64,56},{72,6... | collective-permute-start | bytes 393224 | tf_op jit(solution)/shard_map/ppermute | solution.py:25
  78.9 6.5 %collective-permute-start.15 = (f32[16,18,1,128]{3,0,2,1:T(8,128)S(1)}, f32[16,18,1,128]{3,0,2,1:T(8,128)S(1)}, u32[]{:S(2)}, u32[]{:S(2)}) collective-permute-start(f32[16,18,1,128]{3,0,2,1:T(8,128)S(1)} %get-tuple-element.46), channel_id=1, source_target_pairs={{1,0},{2,1},{3,2},{4,3},{5,4},{6,5},{7,6},{9,8},{10,9},{11,10},{12... | collective-permute-start | bytes 442376 | tf_op jit(solution)/shard_map/ppermute | solution.py:25
  88.7 8.1 %collective-permute-start.16 = (f32[16,1,16,128]{3,0,2,1:T(8,128)S(1)}, f32[16,1,16,128]{3,0,2,1:T(8,128)S(1)}, u32[]{:S(2)}, u32[]{:S(2)}) collective-permute-start(f32[16,1,16,128]{3,0,2,1:T(8,128)S(1)} %get-tuple-element.63), channel_id=1, source_target_pairs={{0,8},{8,16},{16,24},{24,32},{32,40},{40,48},{48,56},{56,64},{64,7... | collective-permute-start | bytes 393224 | tf_op jit(solution)/shard_map/ppermute | solution.py:24
  94.9 6.3 %collective-permute-start.17 = (f32[16,1,16,128]{3,0,2,1:T(8,128)S(1)}, f32[16,1,16,128]{3,0,2,1:T(8,128)S(1)}, u32[]{:S(2)}, u32[]{:S(2)}) collective-permute-start(f32[16,1,16,128]{3,0,2,1:T(8,128)S(1)} %get-tuple-element.64), channel_id=1, source_target_pairs={{8,0},{16,8},{24,16},{32,24},{40,32},{48,40},{56,48},{64,56},{72,6... | collective-permute-start | bytes 393224 | tf_op jit(solution)/shard_map/ppermute | solution.py:25
  104.5 6.5 %collective-permute-start.19 = (f32[16,18,1,128]{3,0,2,1:T(8,128)S(1)}, f32[16,18,1,128]{3,0,2,1:T(8,128)S(1)}, u32[]{:S(2)}, u32[]{:S(2)}) collective-permute-start(f32[16,18,1,128]{3,0,2,1:T(8,128)S(1)} %get-tuple-element.44), channel_id=1, source_target_pairs={{1,0},{2,1},{3,2},{4,3},{5,4},{6,5},{7,6},{9,8},{10,9},{11,10},{12... | collective-permute-start | bytes 442376 | tf_op jit(solution)/shard_map/ppermute | solution.py:25
  117.6 5.8 collective-permute-start.21
  123.4 7.9 %collective-permute-start.22 = (f32[16,18,1,128]{3,0,2,1:T(8,128)S(1)}, f32[16,18,1,128]{3,0,2,1:T(8,128)S(1)}, u32[]{:S(2)}, u32[]{:S(2)}) collective-permute-start(f32[16,18,1,128]{3,0,2,1:T(8,128)S(1)} %get-tuple-element.41), channel_id=1, source_target_pairs={{0,1},{1,2},{2,3},{3,4},{4,5},{5,6},{6,7},{8,9},{9,10},{10,11},{11... | collective-permute-start | bytes 442376 | tf_op jit(solution)/shard_map/ppermute | solution.py:24
  126.6 6.5 %collective-permute-start.23 = (f32[16,18,1,128]{3,0,2,1:T(8,128)S(1)}, f32[16,18,1,128]{3,0,2,1:T(8,128)S(1)}, u32[]{:S(2)}, u32[]{:S(2)}) collective-permute-start(f32[16,18,1,128]{3,0,2,1:T(8,128)S(1)} %get-tuple-element.42), channel_id=1, source_target_pairs={{1,0},{2,1},{3,2},{4,3},{5,4},{6,5},{7,6},{9,8},{10,9},{11,10},{12... | collective-permute-start | bytes 442376 | tf_op jit(solution)/shard_map/ppermute | solution.py:25
  239.6 5.7 collective-permute-start.25
  245.3 6.5 %collective-permute-start.26 = (f32[16,18,1,128]{3,0,2,1:T(8,128)S(1)}, f32[16,18,1,128]{3,0,2,1:T(8,128)S(1)}, u32[]{:S(2)}, u32[]{:S(2)}) collective-permute-start(f32[16,18,1,128]{3,0,2,1:T(8,128)S(1)} %get-tuple-element.39), channel_id=1, source_target_pairs={{0,1},{1,2},{2,3},{3,4},{4,5},{5,6},{6,7},{8,9},{9,10},{10,11},{11... | collective-permute-start | bytes 442376 | tf_op jit(solution)/shard_map/ppermute | solution.py:24
  249.8 6.5 %collective-permute-start.27 = (f32[16,18,1,128]{3,0,2,1:T(8,128)S(1)}, f32[16,18,1,128]{3,0,2,1:T(8,128)S(1)}, u32[]{:S(2)}, u32[]{:S(2)}) collective-permute-start(f32[16,18,1,128]{3,0,2,1:T(8,128)S(1)} %get-tuple-element.40), channel_id=1, source_target_pairs={{1,0},{2,1},{3,2},{4,3},{5,4},{6,5},{7,6},{9,8},{10,9},{11,10},{12... | collective-permute-start | bytes 442376 | tf_op jit(solution)/shard_map/ppermute | solution.py:25
  262.3 6.0 %collective-permute-start.29 = (f32[16,1,16,128]{3,0,2,1:T(8,128)S(1)}, f32[16,1,16,128]{3,0,2,1:T(8,128)S(1)}, u32[]{:S(2)}, u32[]{:S(2)}) collective-permute-start(f32[16,1,16,128]{3,0,2,1:T(8,128)S(1)} %get-tuple-element.58), channel_id=1, source_target_pairs={{8,0},{16,8},{24,16},{32,24},{40,32},{48,40},{56,48},{64,56},{72,6... | collective-permute-start | bytes 393224 | tf_op jit(solution)/shard_map/ppermute | solution.py:25
  268.3 6.2 %collective-permute-start.30 = (f32[16,18,1,128]{3,0,2,1:T(8,128)S(1)}, f32[16,18,1,128]{3,0,2,1:T(8,128)S(1)}, u32[]{:S(2)}, u32[]{:S(2)}) collective-permute-start(f32[16,18,1,128]{3,0,2,1:T(8,128)S(1)} %get-tuple-element.37), channel_id=1, source_target_pairs={{0,1},{1,2},{2,3},{3,4},{4,5},{5,6},{6,7},{8,9},{9,10},{10,11},{11... | collective-permute-start | bytes 442376 | tf_op jit(solution)/shard_map/ppermute | solution.py:24
  272.5 6.5 %collective-permute-start.31 = (f32[16,18,1,128]{3,0,2,1:T(8,128)S(1)}, f32[16,18,1,128]{3,0,2,1:T(8,128)S(1)}, u32[]{:S(2)}, u32[]{:S(2)}) collective-permute-start(f32[16,18,1,128]{3,0,2,1:T(8,128)S(1)} %get-tuple-element.38), channel_id=1, source_target_pairs={{1,0},{2,1},{3,2},{4,3},{5,4},{6,5},{7,6},{9,8},{10,9},{11,10},{12... | collective-permute-start | bytes 442376 | tf_op jit(solution)/shard_map/ppermute | solution.py:25
  291.7 6.7 %collective-permute-start.34 = (f32[16,18,1,128]{3,0,2,1:T(8,128)S(1)}, f32[16,18,1,128]{3,0,2,1:T(8,128)S(1)}, u32[]{:S(2)}, u32[]{:S(2)}) collective-permute-start(f32[16,18,1,128]{3,0,2,1:T(8,128)S(1)} %get-tuple-element.35), channel_id=1, source_target_pairs={{0,1},{1,2},{2,3},{3,4},{4,5},{5,6},{6,7},{8,9},{9,10},{10,11},{11... | collective-permute-start | bytes 442376 | tf_op jit(solution)/shard_map/ppermute | solution.py:24
  296.3 6.5 %collective-permute-start.35 = (f32[16,18,1,128]{3,0,2,1:T(8,128)S(1)}, f32[16,18,1,128]{3,0,2,1:T(8,128)S(1)}, u32[]{:S(2)}, u32[]{:S(2)}) collective-permute-start(f32[16,18,1,128]{3,0,2,1:T(8,128)S(1)} %get-tuple-element.36), channel_id=1, source_target_pairs={{1,0},{2,1},{3,2},{4,3},{5,4},{6,5},{7,6},{9,8},{10,9},{11,10},{12... | collective-permute-start | bytes 442376 | tf_op jit(solution)/shard_map/ppermute | solution.py:25
  397.9 5.8 collective-permute-start.36
  399.2 5.7 collective-permute-start.37
  404.9 9.2 %collective-permute-start.38 = (f32[16,18,1,128]{3,0,2,1:T(8,128)S(1)}, f32[16,18,1,128]{3,0,2,1:T(8,128)S(1)}, u32[]{:S(2)}, u32[]{:S(2)}) collective-permute-start(f32[16,18,1,128]{3,0,2,1:T(8,128)S(1)} %get-tuple-element.33), channel_id=1, source_target_pairs={{0,1},{1,2},{2,3},{3,4},{4,5},{5,6},{6,7},{8,9},{9,10},{10,11},{11... | collective-permute-start | bytes 442376 | tf_op jit(solution)/shard_map/ppermute | solution.py:24
  409.4 6.5 %collective-permute-start.39 = (f32[16,18,1,128]{3,0,2,1:T(8,128)S(1)}, f32[16,18,1,128]{3,0,2,1:T(8,128)S(1)}, u32[]{:S(2)}, u32[]{:S(2)}) collective-permute-start(f32[16,18,1,128]{3,0,2,1:T(8,128)S(1)} %get-tuple-element.34), channel_id=1, source_target_pairs={{1,0},{2,1},{3,2},{4,3},{5,4},{6,5},{7,6},{9,8},{10,9},{11,10},{12... | collective-permute-start | bytes 442376 | tf_op jit(solution)/shard_map/ppermute | solution.py:25
  (18 other events, 278.5 us)
where the time goes:
time: 602 us; the launch traced here: 594 us
  blocking collectives  323 us (54%)
  starting transfers between devices  107 us (18%)
  waiting for transfers between devices  70.1 us (12%)
  other arithmetic  38.4 us (6%)
  matrix products  38 us (6%)
  local copies, waits for them, and re-layouts  15.8 us (3%)
    psum x2, blocking collectives, body(): lax.psum((gram_matrix(direction, mapped), gram_matrix(direction, residual...  168 us
    psum x1, blocking collectives, body(): cross_terms = lax.psum(gram_matrix(mapped, smoothed), ('gx', 'gy'))  82.2 us
    ppermute x20, starting transfers between devices, padded_2(): before = lax.ppermute(last, axis, up)  74.1 us
    psum x1, blocking collectives, body(): lax.psum(jnp.einsum('fxye,pfxy->pe', onehot_faces, surface, precision=lax...  72.7 us
    ppermute x20, waiting for transfers between devices, padded_2(): after = lax.ppermute(initial, axis, down)  64.8 us
    ppermute x20, starting transfers between devices, padded_2(): after = lax.ppermute(initial, axis, down)  32.6 us
    add x6, other arithmetic, chebyshev(): iterate = iterate + update  19.6 us
    dot_general x5, matrix products, gram_matrix(): jnp.einsum('pxyz,qxyz->pq', first_set, second_set, precision=lax.Precisio...  18.1 us
  transfers between devices with their start and end apart: 40, of which 29 were waited for; matrix products, arithmetic and copies ran while one was open for 2% of the time, Pallas kernels for 0%

commit v1 on v0

v1 whole, which is shorter than its diff:
```python
import functools

import jax
import jax.numpy as jnp
import numpy as np
from jax import lax
from jax.experimental import pallas as pl
from jax.experimental.pallas import tpu as pltpu
from jax.sharding import PartitionSpec as P

ELECTRODES = 256
REGIONS = 8
PATCH = 2
SWEEPS = 3
CHEB_LOW = 0.1
CHEB_HIGH = 2.0

PATS = 16
BLK = 16
NZ = 128
DEEP = 9
EXT = BLK + 2 * DEEP
ROWS = 3 * BLK
YOFF = BLK - DEEP
COND = BLK
FACE = BLK + 1
UPPER = 64
CONTACT = 32

F32 = jnp.float32
BF16 = jnp.bfloat16
HIGHEST = lax.Precision.HIGHEST


def polynomial():
    middle = 0.5 * (CHEB_HIGH + CHEB_LOW)
    radius = 0.5 * (CHEB_HIGH - CHEB_LOW)
    sharp = middle / radius
    rho = 1.0 / sharp
    step = np.array([1.0])
    n_of_s = np.array([1.0, -1.0])
    update = np.array([1.0 / middle])
    iterate = update
    for _ in range(SWEEPS):
        defect = np.polynomial.polynomial.polysub(
            step, np.polynomial.polynomial.polymul(n_of_s, iterate)
        )
        rho_next = 1.0 / (2.0 * sharp - rho)
        update = np.polynomial.polynomial.polyadd(
            rho_next * rho * update, 2.0 * rho_next / radius * defect
        )
        iterate = np.polynomial.polynomial.polyadd(iterate, update)
        rho = rho_next
    return [float(v) for v in iterate]


E0, E1, E2, E3 = polynomial()
MIX = (E2 / E3, E1 / E3, E0 / E3)


def corner_blocks():
    rows = [(0, i, DEEP - i) for i in range(1, DEEP)]
    rows += [(1, i, i + 1) for i in range(DEEP - 1)]
    return rows


CORNER = sum(DEEP - k for _, _, k in corner_blocks()) + 2 * len(corner_blocks())


def vmem(mib):
    return pltpu.CompilerParams(vmem_limit_bytes=mib * 1024 * 1024)


VM = pl.BlockSpec(memory_space=pltpu.VMEM)
SM = pl.BlockSpec(memory_space=pltpu.SMEM)


def pack_kernel(side, cond, start, label, texture, face, block, up, down, mate, away):
    side_c = side[0]

    def row(x, carry):
        block[x, 0:BLK] = pltpu.einshape("pyz->ypz", start[:, x])
        lab = label[x]
        value = jnp.zeros((BLK, NZ), F32)
        for region in range(REGIONS):
            value = jnp.where(lab == region, cond[region], value)
        block[x, COND] = value * texture[x]
        block[x, FACE] = face[x]
        return carry

    lax.fori_loop(0, BLK, row, 0)
    base_mate = (BLK - DEEP) * (1 - side_c)
    base_away = (BLK - DEEP) * side_c

    def faces(x, carry):
        for j in range(DEEP):
            mate[x, j] = block[x, base_mate + j]
            away[x, j] = block[x, base_away + j]
        for j in range(2):
            mate[x, DEEP + j] = block[x, COND + j]
            away[x, DEEP + j] = block[x, COND + j]
        return carry

    lax.fori_loop(0, BLK, faces, 0)

    def ends(x, carry):
        for j in range(BLK + 2):
            up[x, j] = block[BLK - DEEP + x, j]
            down[x, j] = block[x, j]
        return carry

    lax.fori_loop(0, DEEP, ends, 0)


def pack(side, region_cond, start, label, texture, face):
    shape = jax.ShapeDtypeStruct
    return pl.pallas_call(
        pack_kernel,
        out_shape=(
            shape((BLK, BLK + 2, PATS, NZ), F32),
            shape((DEEP, BLK + 2, PATS, NZ), F32),
            shape((DEEP, BLK + 2, PATS, NZ), F32),
            shape((BLK, DEEP + 2, PATS, NZ), F32),
            shape((BLK, DEEP + 2, PATS, NZ), F32),
        ),
        in_specs=[SM, SM, VM, VM, VM, VM],
        out_specs=(VM,) * 5,
        compiler_params=vmem(40),
    )(side, region_cond, start, label, texture, face)


def corner_kernel(side, low, high, mate, away):
    side_c = side[0]
    at = 0
    for which, i, k in corner_blocks():
        src = low if which == 0 else high
        count = DEEP - k
        base_mate = (BLK - count) * (1 - side_c)
        base_away = (BLK - count) * side_c
        for j in range(count):
            mate[at] = src[i, base_mate + j]
            away[at] = src[i, base_away + j]
            at += 1
        for j in range(2):
            mate[at] = src[i, COND + j]
            away[at] = src[i, COND + j]
            at += 1


def corners(side, low, high):
    shape = jax.ShapeDtypeStruct((CORNER, PATS, NZ), F32)
    return pl.pallas_call(
        corner_kernel,
        out_shape=(shape, shape),
        in_specs=[SM, VM, VM],
        out_specs=(VM, VM),
        compiler_params=vmem(24),
    )(side, low, high)


def harmonic(own, other):
    total = own + other
    return 2.0 * own * other / jnp.where(total > 0, total, 1.0)


def split(value):
    high = value.astype(BF16)
    return high, (value - high.astype(F32)).astype(BF16)


def split3(value):
    high = value.astype(BF16)
    rest = value - high.astype(F32)
    middle = rest.astype(BF16)
    return high, middle, (rest - middle.astype(F32)).astype(BF16)


def gram(first, seconds, origin):
    width = 2 * PATS * len(seconds)

    def row(i, total):
        x = origin + i

        def flat(ref):
            return jnp.concatenate([ref[x, origin + j] for j in range(BLK)], axis=1)

        left = jnp.concatenate(split(flat(first)), axis=0)
        parts = [split(flat(ref)) for ref in seconds]
        right = jnp.concatenate([p[0] for p in parts] + [p[1] for p in parts], axis=0)
        return total + lax.dot_general(
            left, right, (((1,), (1,)), ((), ())), preferred_element_type=F32
        )

    total = lax.fori_loop(0, BLK, row, jnp.zeros((2 * PATS, width), F32))
    total = total[:PATS] + total[PATS:]
    half = width // 2
    return total[:, :half] + total[:, half:]


def main_kernel(
    side, marks, block, low, high, mate, away, cmate, caway,
    out_u, out_z, out_scale, out_chunk,
    fa, fb, fc, faces, cond, cx, cy, cz, diag, scale, volt,
):
    side_c = side[0]
    lane = lax.broadcasted_iota(jnp.int32, (PATS, NZ), 1)
    first_lane = lane == 0
    last_lane = lane == NZ - 1

    zero = jnp.zeros((PATS, NZ), F32)

    def clear(i, carry):
        for j in range(DEEP):
            fa[i, j] = zero
            fa[i, EXT - 1 - j] = zero
            fa[EXT - 1 - i, j] = zero
            fa[EXT - 1 - i, EXT - 1 - j] = zero
        return carry

    lax.fori_loop(0, DEEP, clear, 0)
    for which in (0, 2):
        for i in (0, EXT - 1):
            faces[i, which] = zero
            cond[i, which * BLK : (which + 1) * BLK] = zero

    def put_row(dst, src, x):
        for j in range(BLK):
            fa[dst, DEEP + j] = src[x, j]
        cond[dst, BLK : 2 * BLK] = src[x, COND]
        faces[dst, 1] = src[x, FACE]

    def own_rows(x, carry):
        put_row(DEEP + x, block, x)
        return carry

    def halo_rows(x, carry):
        put_row(x, low, x)
        put_row(DEEP + BLK + x, high, x)
        return carry

    lax.fori_loop(0, BLK, own_rows, 0)
    lax.fori_loop(0, DEEP, halo_rows, 0)

    def put_sides(below, above, cbelow, cabove):
        def side_rows(x, carry):
            for j in range(DEEP):
                fa[DEEP + x, j] = below[x, j]
                fa[DEEP + x, DEEP + BLK + j] = above[x, j]
            for src, which in ((below, 0), (above, 2)):
                cond[DEEP + x, which * BLK : (which + 1) * BLK] = src[x, DEEP]
                faces[DEEP + x, which] = src[x, DEEP + 1]
            return carry

        lax.fori_loop(0, BLK, side_rows, 0)
        at = 0
        for which_x, i, k in corner_blocks():
            x = i if which_x == 0 else DEEP + BLK + i
            for j in range(DEEP - k):
                fa[x, k + j] = cbelow[at]
                fa[x, DEEP + BLK + j] = cabove[at]
                at += 1
            for src, which in ((cbelow, 0), (cabove, 2)):
                cond[x, which * BLK : (which + 1) * BLK] = src[at]
                faces[x, which] = src[at + 1]
            at += 2

    @pl.when(side_c == 0)
    def _():
        put_sides(away, mate, caway, cmate)

    @pl.when(side_c == 1)
    def _():
        put_sides(mate, away, cmate, caway)

    wide_lane = lax.broadcasted_iota(jnp.int32, (ROWS, NZ), 1)

    def conductances(x, carry):
        here = cond[x]
        cx[x] = harmonic(here, cond[jnp.minimum(x + 1, EXT - 1)])
        cy[x] = harmonic(here, pltpu.roll(here, ROWS - 1, 0))
        cz[x] = jnp.where(
            wide_lane == NZ - 1, 0.0, harmonic(here, pltpu.roll(here, NZ - 1, 1))
        )
        return carry

    lax.fori_loop(0, EXT, conductances, 0)

    def diagonals(x, carry):
        face = jnp.concatenate([faces[x, 0], faces[x, 1], faces[x, 2]], axis=0)
        contact = jnp.where(
            wide_lane == 0,
            pltpu.roll(face, NZ - CONTACT, 1),
            jnp.where(
                wide_lane == NZ - 1, pltpu.roll(face, NZ - 2 - CONTACT, 1), 0.0
            ),
        )
        own_y = cy[x]
        own_z = cz[x]
        total = (
            contact
            + cx[x]
            + cx[jnp.maximum(x - 1, 0)]
            + own_y
            + pltpu.roll(own_y, 1, 0)
            + own_z
            + pltpu.roll(own_z, 1, 1)
        )
        positive = total > 0
        diag[x] = total
        scale[x] = jnp.where(positive, lax.rsqrt(jnp.where(positive, total, 1.0)), 0.0)
        return carry

    lax.fori_loop(0, EXT, diagonals, 0)

    def at_row(ref, x, y):
        return ref[x, pl.ds(y + YOFF, 1), :]

    def neighbours(src, x, y, below, here, above):
        weight = at_row(cz, x, y)
        return (
            at_row(cx, x - 1, y) * src[x - 1, y]
            + at_row(cx, x, y) * src[x + 1, y]
            + at_row(cy, x, y - 1) * below
            + at_row(cy, x, y) * above
            + weight * pltpu.roll(here, NZ - 1, 1)
            + pltpu.roll(weight * here, 1, 1)
        )

    def sweep(radius, src, finish):
        lo, hi = DEEP - radius, DEEP + BLK + radius

        def row(x, carry):
            below, here = src[x, lo - 1], src[x, lo]
            for y in range(lo, hi):
                above = src[x, y + 1]
                finish(x, y, here, neighbours(src, x, y, below, here, above))
                below, here = here, above
            return carry

        lax.fori_loop(lo, hi, row, 0)

    def residual(x, y, here, total):
        which, spot = (
            (0, y + YOFF) if y < DEEP
            else (1, y - DEEP) if y < DEEP + BLK
            else (2, y - DEEP - BLK)
        )
        face = faces[x, which]
        source = jnp.where(
            first_lane,
            pltpu.roll(face, (NZ - spot) % NZ, 1),
            jnp.where(last_lane, pltpu.roll(face, NZ - 1 - UPPER - spot, 1), 0.0),
        )
        fb[x, y] = at_row(scale, x, y) * (source - at_row(diag, x, y) * here + total)

    sweep(DEEP - 1, fa, residual)

    def rescale(x, carry):
        here = scale[x]
        cx[x] = cx[x] * here * scale[jnp.minimum(x + 1, EXT - 1)]
        cy[x] = cy[x] * here * pltpu.roll(here, ROWS - 1, 0)
        cz[x] = cz[x] * here * pltpu.roll(here, NZ - 1, 1)
        return carry

    lax.fori_loop(0, EXT, rescale, 0)

    def mixed(dst, base, factor):
        def finish(x, y, here, total):
            dst[x, y] = factor * base[x, y] + total

        return finish

    def mapped(dst):
        def finish(x, y, here, total):
            dst[x, y] = here - total

        return finish

    def smooth(radius, base, one, two):
        sweep(radius + 2, base, mixed(one, base, MIX[0]))
        sweep(radius + 1, one, mixed(two, base, MIX[1]))
        sweep(radius, two, mixed(one, base, MIX[2]))

    smooth(5, fb, fa, fc)
    sweep(4, fa, mapped(fc))
    gram_first = gram(fa, (fb, fc), DEEP)

    def save(dst, src):
        def row(x, carry):
            for y in range(BLK):
                dst[x, y] = src[DEEP + x, DEEP + y]
            return carry

        lax.fori_loop(0, BLK, row, 0)

    save(out_u, fa)
    smooth(1, fc, fb, fa)
    sweep(0, fb, mapped(fa))
    gram_second = gram(fb, (fc, fa), DEEP)
    save(out_z, fb)

    def save_scale(x, carry):
        out_scale[x] = scale[DEEP + x, BLK : 2 * BLK]
        return carry

    lax.fori_loop(0, BLK, save_scale, 0)

    volt[...] = jnp.zeros_like(volt)
    elane = lax.broadcasted_iota(jnp.int32, (PATS, ELECTRODES), 1)
    half = BLK // PATCH

    def electrode(i, carry):
        mark = marks[i]

        @pl.when(mark > 0)
        def _():
            face = i // (half * half)
            x0 = (i // half) % half * PATCH
            y0 = i % half * PATCH
            wanted = lane == face * (NZ - 1)
            sums = [zero, zero, zero]
            for dx in range(PATCH):
                for dy in range(PATCH):
                    x, y = x0 + dx, y0 + dy
                    weight = out_scale[x, pl.ds(y, 1), :]
                    sums[0] += block[x, y]
                    sums[1] += weight * out_u[x, y]
                    sums[2] += weight * out_z[x, y]
            for f in range(3):
                total = jnp.sum(jnp.where(wanted, sums[f], 0.0), axis=1, keepdims=True)
                volt[f] = volt[f] + jnp.where(elane == mark - 1, total, 0.0)

        return carry

    lax.fori_loop(0, 2 * half * half, electrode, 0)

    grams = jnp.concatenate(
        [gram_first, gram_second, jnp.zeros((PATS, NZ - 4 * PATS), F32)], axis=1
    )
    per = ELECTRODES // 8
    for d in range(8):
        tile, spot = d * per // NZ, d * per % NZ
        picked = zero
        for f in range(3):
            part = volt[f, :, tile * NZ : (tile + 1) * NZ]
            part = pltpu.roll(part, (per * f - spot) % NZ, 1)
            inside = (lane >= per * f) & (lane < per * (f + 1))
            picked = jnp.where(inside, part, picked)
        out_chunk[d, 0:PATS] = picked
        out_chunk[d, PATS : 2 * PATS] = grams


def main_call(side, marks, block, low, high, mate, away, cmate, caway):
    shape = jax.ShapeDtypeStruct
    field = pltpu.VMEM((EXT, EXT, PATS, NZ), F32)
    plane = pltpu.VMEM((EXT, ROWS, NZ), F32)
    return pl.pallas_call(
        main_kernel,
        out_shape=(
            shape((BLK, BLK, PATS, NZ), F32),
            shape((BLK, BLK, PATS, NZ), F32),
            shape((BLK, BLK, NZ), F32),
            shape((8, 2 * PATS, NZ), F32),
        ),
        in_specs=[SM, SM] + [VM] * 7,
        out_specs=(VM,) * 4,
        scratch_shapes=[
            field, field, field,
            pltpu.VMEM((EXT, 3, PATS, NZ), F32),
            plane, plane, plane, plane, plane, plane,
            pltpu.VMEM((3, PATS, ELECTRODES), F32),
        ],
        compiler_params=vmem(60),
    )(side, marks, block, low, high, mate, away, cmate, caway)


def solve_kernel(parts, out_mix, out_volt):
    volts = parts[0, 0:PATS]
    grams = parts[0, PATS : 2 * PATS]
    for i in range(1, parts.shape[0]):
        volts = volts + parts[i, 0:PATS]
        grams = grams + parts[i, PATS : 2 * PATS]
    lane = lax.broadcasted_iota(jnp.int32, (PATS, NZ), 1)

    a_at, b_at, c_at, e_at = 0, PATS, 2 * PATS, 3 * PATS

    def move(source, target):
        return pltpu.roll(grams, (target - source) % NZ, 1)

    def pick(first, second, third):
        return jnp.where(
            lane < PATS,
            move(first, 0),
            jnp.where(
                lane < 2 * PATS,
                move(second, PATS),
                jnp.where(lane < 3 * PATS, move(third, 2 * PATS), 0.0),
            ),
        )

    table = jnp.concatenate([pick(b_at, c_at, a_at), pick(c_at, e_at, b_at)], axis=0)
    rows = lax.broadcasted_iota(jnp.int32, (2 * PATS, NZ), 0)
    for k in range(2 * PATS):
        pivot = table[k : k + 1] / table[k : k + 1, k : k + 1]
        table = jnp.where(rows == k, pivot, table - table[:, k : k + 1] * pivot)
    mix = table[:, 2 * PATS : 3 * PATS]
    eye = (
        lax.broadcasted_iota(jnp.int32, (PATS, PATS), 0)
        == lax.broadcasted_iota(jnp.int32, (PATS, PATS), 1)
    ).astype(F32)
    turned = lax.dot_general(
        eye, mix, (((1,), (1,)), ((), ())), precision=HIGHEST, preferred_element_type=F32
    )
    out_mix[...] = turned
    per = ELECTRODES // 8
    fields = jnp.concatenate(
        [pltpu.roll(volts, NZ - per, 1), pltpu.roll(volts, NZ - 2 * per, 1)], axis=0
    )
    total = volts + jnp.dot(turned, fields, precision=HIGHEST, preferred_element_type=F32)
    out_volt[...] = total * (1.0 / (PATCH * PATCH))


def solve_small(parts):
    shape = jax.ShapeDtypeStruct
    return pl.pallas_call(
        solve_kernel,
        out_shape=(shape((PATS, 2 * PATS), F32), shape((PATS, NZ), F32)),
        in_specs=[VM],
        out_specs=(VM, VM),
        compiler_params=vmem(16),
    )(parts)


def update_kernel(mix, start, u, z, scale, out):
    left = jnp.concatenate(
        [jnp.concatenate([part] * 3, axis=1) for part in split3(mix[...])], axis=0
    )

    def row(x, carry):
        data = jnp.concatenate(
            [
                jnp.concatenate([u[x, y] for y in range(BLK)], axis=1),
                jnp.concatenate([z[x, y] for y in range(BLK)], axis=1),
            ],
            axis=0,
        )
        right = jnp.concatenate(split3(data), axis=0)
        both = jnp.dot(left, right, preferred_element_type=F32)
        both = both[:PATS] + (both[PATS : 2 * PATS] + both[2 * PATS :])
        change = jnp.stack(
            [
                both[:, y * NZ : (y + 1) * NZ] * scale[x, pl.ds(y, 1), :]
                for y in range(BLK)
            ],
            axis=0,
        )
        out[:, x] = start[:, x] + pltpu.einshape("ypz->pyz", change)
        return carry

    lax.fori_loop(0, BLK, row, 0)


def update(mix, start, u, z, scale):
    return pl.pallas_call(
        update_kernel,
        out_shape=jax.ShapeDtypeStruct(start.shape, F32),
        in_specs=[VM] * 5,
        out_specs=VM,
        compiler_params=vmem(24),
    )(mix, start, u, z, scale)


def face_blocks(electrode_map, currents, contact_gain):
    numbers = jnp.arange(1, ELECTRODES + 1, dtype=jnp.int32)
    onehot = (electrode_map[..., None] == numbers).astype(F32)
    contact = jnp.einsum("fxye,e->xyf", onehot, contact_gain, precision=HIGHEST)
    source = jnp.einsum("fxye,ep->fxpy", onehot, currents, precision=HIGHEST)
    gap = lambda width: jnp.zeros((BLK, PATS, width), F32)
    return jnp.concatenate(
        [
            source[0], gap(CONTACT - BLK), contact, gap(UPPER - CONTACT - 2),
            source[1], gap(NZ - UPPER - BLK),
        ],
        axis=2,
    )


def body(start_field, currents, electrode_map, contact_gain, region_label, region_cond, texture):
    gx, gy = lax.axis_size("gx"), lax.axis_size("gy")
    side = (lax.axis_index("gy") % 2).astype(jnp.int32).reshape(1)
    marks = electrode_map[:, ::PATCH, ::PATCH].reshape(-1)
    face = face_blocks(electrode_map, currents, contact_gain)
    block, up, down, mate, away = pack(
        side, region_cond, start_field, region_label, texture, face
    )
    rise = [(i, i + 1) for i in range(gx - 1)]
    fall = [(j, i) for i, j in rise]
    pairs = [(i, i + 1) for i in range(0, gy, 2)]
    gaps = [(i, i + 1) for i in range(1, gy - 1, 2)]
    within = pairs + [(j, i) for i, j in pairs]
    across = gaps + [(j, i) for i, j in gaps]
    low = lax.ppermute(up, "gx", rise)
    high = lax.ppermute(down, "gx", fall)
    away = lax.ppermute(away, "gy", across)
    mate = lax.ppermute(mate, "gy", within)
    cmate, caway = corners(side, low, high)
    caway = lax.ppermute(caway, "gy", across)
    cmate = lax.ppermute(cmate, "gy", within)
    u, z, scale, chunk = main_call(
        side, marks, block, low, high, mate, away, cmate, caway
    )
    chunk = lax.all_to_all(chunk, "gy", 0, 0, tiled=True)
    chunk = jnp.sum(chunk, axis=0)
    parts = jnp.broadcast_to(chunk[None], (gx,) + chunk.shape)
    parts = lax.all_to_all(parts, "gx", 0, 0, tiled=True)
    mix, volt = solve_small(parts)
    volts = jnp.broadcast_to(volt[None], (gy,) + volt.shape)
    volts = lax.all_to_all(volts, "gy", 0, 0, tiled=True)
    result = update(mix, start_field, u, z, scale)
    per = ELECTRODES // gy
    voltages = volts[:, :, :per].transpose(1, 0, 2).reshape(PATS, ELECTRODES)
    return result, voltages


def solution(mesh):
    placed = (
        P(None, "gx", "gy", None),
        P(),
        P(None, "gx", "gy"),
        P(),
        P("gx", "gy", None),
        P(),
        P("gx", "gy", None),
    )
    return jax.shard_map(
        body,
        mesh=mesh,
        in_specs=placed,
        out_specs=(P(None, "gx", "gy", None), P()),
        check_vma=False,
    )
```

time: 602 us -> 190 us (0.32); the launches traced: 594 us -> 189 us
  blocking collectives: 323 us -> 38.3 us
  starting transfers between devices: 107 us -> 21.1 us
  Pallas kernels: 0 us -> 80.3 us
  other arithmetic: 38.4 us -> 0.02 us
  matrix products: 38 us -> 3.77 us
  waiting for transfers between devices: 70.1 us -> 36.6 us
  local copies, waits for them, and re-layouts: 15.8 us -> 8.33 us
    psum x4 -> x0, blocking collectives: 323 us -> none  [the longest x2 168 us: body(): lax.psum((gram_matrix(direction, mapped), gram_matrix(direction, residual...]
    ppermute x40 -> x6, starting transfers between devices: 107 us -> 14.5 us  [the longest x1 4.15 us: body(): low = lax.ppermute(up, 'gx', rise)]
    pallas_call x0 -> x5, Pallas kernels: none -> 80.3 us  [the longest x1 67.7 us: main_call(): pl.pallas_call(main_kernel, out_shape=(shape((BLK, BLK, PATS, NZ), F32),...]
    all_to_all x0 -> x2, blocking collectives: none -> 38.3 us  [the longest x1 28.2 us: body(): parts = lax.all_to_all(parts, 'gx', 0, 0, tiled=True)]
    ppermute x40 -> x6, waiting for transfers between devices: 70.1 us -> 36.6 us  [the longest x1 22.2 us: body(): low = lax.ppermute(up, 'gx', rise)]
    dot_general x12 -> x2, matrix products: 36.9 us -> 3.77 us  [the longest x1 1.95 us: face_blocks(): contact = jnp.einsum('fxye,e->xyf', onehot, contact_gain, precision=HIGHEST)]
    add x8 -> x1, other arithmetic: 23.2 us -> 0.01 us  [face_blocks(): numbers = jnp.arange(1, ELECTRODES + 1, dtype=jnp.int32)]
    another operation x10 -> x0, other arithmetic: 8.01 us -> none  [the longest x6 4.26 us: body(): factor = jnp.linalg.cholesky(curvature)]
  transfers between devices with their start and end apart: 40 -> 7, of which waited for: 29 -> 3; matrix products, arithmetic and copies ran while one was open for 2% -> 0% of each run, Pallas kernels for 0% -> 3%
where the time goes in v1:
time: 190 us; the launch traced here: 189 us
  Pallas kernels  80.3 us (42%)
  blocking collectives  38.3 us (20%)
  waiting for transfers between devices  36.6 us (19%)
  starting transfers between devices  21.1 us (11%)
  local copies, waits for them, and re-layouts  8.33 us (4%)
  matrix products  3.77 us (2%)
    pallas_call x1, Pallas kernels, main_call(): pl.pallas_call(main_kernel, out_shape=(shape((BLK, BLK, PATS, NZ), F32),...  67.7 us
    all_to_all x1, blocking collectives, body(): parts = lax.all_to_all(parts, 'gx', 0, 0, tiled=True)  28.2 us
    ppermute x1, waiting for transfers between devices, body(): low = lax.ppermute(up, 'gx', rise)  22.2 us
    ppermute x1, waiting for transfers between devices, body(): caway = lax.ppermute(caway, 'gy', across)  10.5 us
    all_to_all x1, blocking collectives, body(): chunk = lax.all_to_all(chunk, 'gy', 0, 0, tiled=True)  10.1 us
    all_to_all x1, starting transfers between devices, body(): volts = lax.all_to_all(volts, 'gy', 0, 0, tiled=True)  6.54 us
    unnamed x24, local copies, waits for them, and re-layouts  5.72 us
    pallas_call x1, Pallas kernels, update(): pl.pallas_call(update_kernel, out_shape=jax.ShapeDtypeStruct(start.shape,...  4.99 us
  transfers between devices with their start and end apart: 7, of which 3 were waited for; matrix products, arithmetic and copies ran while one was open for 0% of the time, Pallas kernels for 3%

profile of v1, /device:TPU:1, one launch (start us, length us, event | category | flops | bytes accessed | tf_op | source)
XLA Modules:
  0.0 189.3 jit_solution(14175115935291536321)
XLA Ops:
  0.6 0.0 copy-start
  0.7 1.9 %fusion = f32[1,2,16,16]{3,0,2,1:T(1,128)S(1)} fusion(f32[256,1,1,1]{0,1,3,2:T(1,128)} %bitcast.22, s32[256]{0:T(256)S(1)} %iota_add_fusion, s32[2,16,16]{2,1,0:T(8,128)} %param.9), kind=kOutput, calls=%fused_computation.1 | convolution fusion | flops 1703936 | bytes 6144 | tf_op jit(solution)/shard_map/fxye,e->xyf/dot_general | solution.py:576
  2.7 0.2 copy.12
  2.8 1.8 convolution_bitcast_fusion
  4.8 0.2 concatenate.3.face
  5.0 3.1 %shard_map.86 = (f32[16,18,16,128]{3,2,1,0:T(8,128)S(1)}, f32[9,18,16,128]{3,2,1,0:T(8,128)S(1)}, f32[9,18,16,128]{3,2,1,0:T(8,128)S(1)}, f32[16,11,16,128]{3,2,1,0:T(8,128)}, f32[16,11,16,128]{3,2,1,0:T(8,128)}) custom-call(s32[1]{0:T(128)} %bitcast.side, f32[8]{0:T(128)S(1)} %copy-done.10, f32[16,16,16,128]{3,2,1,0:T(8,128)S(1)} %copy-done.1, ...), custom_call_target="tpu_custom_call" | custom-call | tf_op jit(solution)/shard_map/pallas_call | solution.py:117
  8.2 1.4 copy-done.4
  9.6 4.1 %collective-permute-start = (f32[9,18,16,128]{3,2,1,0:T(8,128)S(1)}, f32[9,18,16,128]{3,2,1,0:T(8,128)S(1)}, u32[]{:S(2)}, u32[]{:S(2)}) collective-permute-start(f32[9,18,16,128]{3,2,1,0:T(8,128)S(1)} %get-tuple-element.16), channel_id=1, source_target_pairs={{0,8},{8,16},{16,24},{24,32},{32,40},{40,48},{48,56},{56,64},{64,7... | collective-permute-start | bytes 3981320 | tf_op jit(solution)/shard_map/ppermute | solution.py:602
  13.8 1.3 collective-permute-start.1
  15.1 1.0 collective-permute-start.2
  16.1 3.1 %collective-permute-start.3 = (f32[16,11,16,128]{3,2,1,0:T(8,128)}, f32[16,11,16,128]{3,2,1,0:T(8,128)}, u32[]{:S(2)}, u32[]{:S(2)}) collective-permute-start(f32[16,11,16,128]{3,2,1,0:T(8,128)} %get-tuple-element.19), channel_id=1, source_target_pairs={{1,2},{3,4},{5,6},{2,1},{4,3},{6,5},{9,10},{11,12},{13,14},{10,9},... | collective-permute-start | bytes 4325384 | tf_op jit(solution)/shard_map/ppermute | solution.py:604
  19.2 22.2 %collective-permute-done.low = f32[9,18,16,128]{3,2,1,0:T(8,128)S(1)} collective-permute-done((f32[9,18,16,128]{3,2,1,0:T(8,128)S(1)}, f32[9,18,16,128]{3,2,1,0:T(8,128)S(1)}, u32[]{:S(2)}, u32[]{:S(2)}) %collective-permute-start) | collective-permute-done | bytes 1327136 | tf_op jit(solution)/shard_map/ppermute | solution.py:602
  41.5 3.9 %collective-permute-done.1.high = f32[9,18,16,128]{3,2,1,0:T(8,128)S(1)} collective-permute-done((f32[9,18,16,128]{3,2,1,0:T(8,128)S(1)}, f32[9,18,16,128]{3,2,1,0:T(8,128)S(1)}, u32[]{:S(2)}, u32[]{:S(2)}) %collective-permute-start.1) | collective-permute-done | bytes 1327136 | tf_op jit(solution)/shard_map/ppermute | solution.py:603
  45.4 1.3 shard_map.87
  46.7 1.1 copy-done.3
  47.8 1.9 collective-permute-start.4
  49.6 3.1 %collective-permute-start.5 = (f32[104,16,128]{2,1,0:T(8,128)}, f32[104,16,128]{2,1,0:T(8,128)}, u32[]{:S(2)}, u32[]{:S(2)}) collective-permute-start(f32[104,16,128]{2,1,0:T(8,128)} %get-tuple-element.21), channel_id=1, source_target_pairs={{1,2},{3,4},{5,6},{2,1},{4,3},{6,5},{9,10},{11,12},{13,14},{10,9},... | collective-permute-start | bytes 2555912 | tf_op jit(solution)/shard_map/ppermute | solution.py:607
  52.7 0.1 slice.12
  52.8 0.6 reshape.21.marks
  53.4 0.0 collective-permute-done.2.mate
  53.4 10.5 %collective-permute-done.5.caway = f32[104,16,128]{2,1,0:T(8,128)} collective-permute-done((f32[104,16,128]{2,1,0:T(8,128)}, f32[104,16,128]{2,1,0:T(8,128)}, u32[]{:S(2)}, u32[]{:S(2)}) %collective-permute-start.5) | collective-permute-done | bytes 852000 | tf_op jit(solution)/shard_map/ppermute | solution.py:607
  63.9 67.7 %shard_map.88 = (f32[16,16,16,128]{3,2,1,0:T(8,128)}, f32[16,16,16,128]{3,2,1,0:T(8,128)}, f32[16,16,128]{2,1,0:T(8,128)}, f32[8,32,128]{2,1,0:T(8,128)}) custom-call(s32[1]{0:T(128)} %bitcast.side, s32[128]{0:T(128)} %reshape.21.marks, f32[16,18,16,128]{3,2,1,0:T(8,128)} %copy-done.4, f32[9,18,16,128]{3,2,1,0:T(8,128)} %copy-done.2, ...), custom_call_target="tpu_custom_call" | custom-call | tf_op jit(solution)/shard_map/pallas_call | solution.py:457
  131.7 10.1 %all_to_all.15 = f32[8,32,128]{2,1,0:T(8,128)S(1)} all-to-all(f32[8,32,128]{2,1,0:T(8,128)} %get-tuple-element.22), channel_id=1, replica_groups=mesh['gx'=32,'gy'=8] {'gy'}, dimensions={0} | all-to-all | bytes 262144 | tf_op jit(solution)/shard_map/all_to_all | solution.py:612
  141.7 0.1 broadcast_in_dim.26
  141.8 28.2 %all_to_all.16.parts = f32[32,32,128]{2,1,0:T(8,128)S(1)} all-to-all(f32[32,32,128]{2,1,0:T(8,128)S(1)} %broadcast_in_dim.26), channel_id=1, replica_groups=mesh['gx'=32,'gy'=8] {'gx'}, dimensions={0} | all-to-all | bytes 1048576 | tf_op jit(solution)/shard_map/all_to_all | solution.py:615
  170.0 3.1 %shard_map.89 = (f32[16,32]{1,0:T(8,128)S(1)}, f32[16,128]{1,0:T(8,128)S(1)}) custom-call(f32[32,32,128]{2,1,0:T(8,128)S(1)} %all_to_all.16.parts), custom_call_target="tpu_custom_call" | custom-call | tf_op jit(solution)/shard_map/pallas_call | solution.py:525
  173.2 0.6 broadcast_in_dim.27
  173.8 6.5 %all-to-all-start.2 = ((f32[8,16,128]{2,1,0:T(8,128)}), f32[8,16,128]{2,1,0:T(8,128)S(1)}, u32[]{:S(2)}, u32[]{:S(2)}) async-start(f32[8,16,128]{2,1,0:T(8,128)} %broadcast_in_dim.27), calls=%async_computation.2 | async-start | bytes 131072 | tf_op jit(solution)/shard_map/all_to_all | solution.py:618
  180.4 1.6 copy-done.5
  182.0 1.6 copy-done.6
  183.5 5.0 %shard_map.90 = f32[16,16,16,128]{3,2,1,0:T(8,128)} custom-call(f32[16,32]{1,0:T(8,128)S(1)} %get-tuple-element.23.mix, f32[16,16,16,128]{3,2,1,0:T(8,128)S(1)} %copy-done.1, f32[16,16,16,128]{3,2,1,0:T(8,128)S(1)} %copy-done.5, f32[16,16,16,128]{3,2,1,0:T(8,128)S(1)} %copy-done.6, f32[16,16,128]{2,1,0:T(8,128)S(1)} %copy-done.7), custom_call_target="tpu_custom_call" | custom-call | tf_op jit(solution)/shard_map/pallas_call | solution.py:564
  188.6 0.7 reshape.22
  (30 shorter events, 0.1 us)
Async XLA Ops:
  0.6 2.2 %copy-start = (f32[256,16]{0,1:T(8,128)S(1)}, f32[256,16]{0,1:T(8,128)}, u32[]{:S(2)}) copy-start(f32[256,16]{0,1:T(8,128)} %param.8) | copy-start | bytes 49156
  0.6 4.4 %copy-start.1 = (f32[16,16,16,128]{3,2,1,0:T(8,128)S(1)}, f32[16,16,16,128]{3,2,1,0:T(8,128)}, u32[]{:S(2)}) copy-start(f32[16,16,16,128]{3,2,1,0:T(8,128)} %start.3) | copy-start | bytes 6291460
  0.7 4.4 %copy-start.9 = (f32[16,16,128]{2,1,0:T(8,128)S(1)}, f32[16,16,128]{2,1,0:T(8,128)}, u32[]{:S(2)}) copy-start(f32[16,16,128]{2,1,0:T(8,128)} %texture.1) | copy-start | bytes 393220
  0.7 4.4 %copy-start.10 = (f32[8]{0:T(128)S(1)}, f32[8]{0:T(128)}, u32[]{:S(2)}) copy-start(f32[8]{0:T(128)} %cond.1) | copy-start | bytes 100
  0.7 4.4 %copy-start.8 = (s32[16,16,128]{2,1,0:T(8,128)S(1)}, s32[16,16,128]{2,1,0:T(8,128)}, u32[]{:S(2)}) copy-start(s32[16,16,128]{2,1,0:T(8,128)} %label.1) | copy-start | bytes 393220
  8.2 1.4 copy-start.4
  9.6 43.1 %copy-start.11 = (s32[2,16,16]{2,1,0:T(8,128)S(1)}, s32[2,16,16]{2,1,0:T(8,128)}, u32[]{:S(2)}) copy-start(s32[2,16,16]{2,1,0:T(8,128)} %param.9) | copy-start | bytes 6148
  9.6 31.9 %collective-permute-start = (f32[9,18,16,128]{3,2,1,0:T(8,128)S(1)}, f32[9,18,16,128]{3,2,1,0:T(8,128)S(1)}, u32[]{:S(2)}, u32[]{:S(2)}) collective-permute-start(f32[9,18,16,128]{3,2,1,0:T(8,128)S(1)} %get-tuple-element.16), channel_id=1, source_target_pairs={{0,8},{8,16},{16,24},{24,32},{32,40},{40,48},{48,56},{56,64},{64,7... | collective-permute-start | bytes 3981320 | tf_op jit(solution)/shard_map/ppermute | solution.py:602
  13.8 31.6 %collective-permute-start.1 = (f32[9,18,16,128]{3,2,1,0:T(8,128)S(1)}, f32[9,18,16,128]{3,2,1,0:T(8,128)S(1)}, u32[]{:S(2)}, u32[]{:S(2)}) collective-permute-start(f32[9,18,16,128]{3,2,1,0:T(8,128)S(1)} %get-tuple-element.17), channel_id=1, source_target_pairs={{8,0},{16,8},{24,16},{32,24},{40,32},{48,40},{56,48},{64,56},{72,6... | collective-permute-start | bytes 3981320 | tf_op jit(solution)/shard_map/ppermute | solution.py:603
  15.1 38.4 %collective-permute-start.2 = (f32[16,11,16,128]{3,2,1,0:T(8,128)}, f32[16,11,16,128]{3,2,1,0:T(8,128)}, u32[]{:S(2)}, u32[]{:S(2)}) collective-permute-start(f32[16,11,16,128]{3,2,1,0:T(8,128)} %get-tuple-element.18), channel_id=1, source_target_pairs={{0,1},{2,3},{4,5},{6,7},{1,0},{3,2},{5,4},{7,6},{8,9},{10,11},{12,... | collective-permute-start | bytes 4325384 | tf_op jit(solution)/shard_map/ppermute | solution.py:605
  16.1 37.3 %collective-permute-start.3 = (f32[16,11,16,128]{3,2,1,0:T(8,128)}, f32[16,11,16,128]{3,2,1,0:T(8,128)}, u32[]{:S(2)}, u32[]{:S(2)}) collective-permute-start(f32[16,11,16,128]{3,2,1,0:T(8,128)} %get-tuple-element.19), channel_id=1, source_target_pairs={{1,2},{3,4},{5,6},{2,1},{4,3},{6,5},{9,10},{11,12},{13,14},{10,9},... | collective-permute-start | bytes 4325384 | tf_op jit(solution)/shard_map/ppermute | solution.py:604
  41.5 22.5 %copy-start.2 = (f32[9,18,16,128]{3,2,1,0:T(8,128)}, f32[9,18,16,128]{3,2,1,0:T(8,128)S(1)}, u32[]{:S(2)}) copy-start(f32[9,18,16,128]{3,2,1,0:T(8,128)S(1)} %collective-permute-done.low) | copy-start | bytes 3981316
  46.7 1.1 copy-start.3
  47.8 5.7 %collective-permute-start.4 = (f32[104,16,128]{2,1,0:T(8,128)}, f32[104,16,128]{2,1,0:T(8,128)}, u32[]{:S(2)}, u32[]{:S(2)}) collective-permute-start(f32[104,16,128]{2,1,0:T(8,128)} %get-tuple-element.20), channel_id=1, source_target_pairs={{0,1},{2,3},{4,5},{6,7},{1,0},{3,2},{5,4},{7,6},{8,9},{10,11},{12,... | collective-permute-start | bytes 2555912 | tf_op jit(solution)/shard_map/ppermute | solution.py:608
  49.6 14.3 %collective-permute-start.5 = (f32[104,16,128]{2,1,0:T(8,128)}, f32[104,16,128]{2,1,0:T(8,128)}, u32[]{:S(2)}, u32[]{:S(2)}) collective-permute-start(f32[104,16,128]{2,1,0:T(8,128)} %get-tuple-element.21), channel_id=1, source_target_pairs={{1,2},{3,4},{5,6},{2,1},{4,3},{6,5},{9,10},{11,12},{13,14},{10,9},... | collective-permute-start | bytes 2555912 | tf_op jit(solution)/shard_map/ppermute | solution.py:607
  131.7 48.7 %copy-start.7 = (f32[16,16,128]{2,1,0:T(8,128)S(1)}, f32[16,16,128]{2,1,0:T(8,128)}, u32[]{:S(2)}) copy-start(f32[16,16,128]{2,1,0:T(8,128)} %get-tuple-element.26.scale) | copy-start | bytes 393220
  173.8 14.7 %all-to-all-start.2 = ((f32[8,16,128]{2,1,0:T(8,128)}), f32[8,16,128]{2,1,0:T(8,128)S(1)}, u32[]{:S(2)}, u32[]{:S(2)}) async-start(f32[8,16,128]{2,1,0:T(8,128)} %broadcast_in_dim.27), calls=%async_computation.2 | async-start | bytes 131072 | tf_op jit(solution)/shard_map/all_to_all | solution.py:618
  180.4 1.6 copy-start.5
  181.9 1.6 copy-start.6

commit v2 on v1

--- a/solution.py
+++ b/solution.py
@@ -6,7 +6,7 @@
 from jax import lax
 from jax.experimental import pallas as pl
 from jax.experimental.pallas import tpu as pltpu
-from jax.sharding import PartitionSpec as P
+from jax.sharding import Mesh, PartitionSpec as P
 
 ELECTRODES = 256
 REGIONS = 8
@@ -15,6 +15,8 @@
 CHEB_LOW = 0.1
 CHEB_HIGH = 2.0
 
+GX = ("z", "x")
+GY = ("y", "c")
 PATS = 16
 BLK = 16
 NZ = 128
@@ -26,6 +28,8 @@
 FACE = BLK + 1
 UPPER = 64
 CONTACT = 32
+MARK = 34
+MARKROWS = 40
 
 F32 = jnp.float32
 BF16 = jnp.bfloat16
@@ -72,10 +76,13 @@
 
 
 VM = pl.BlockSpec(memory_space=pltpu.VMEM)
+HB = pl.BlockSpec(memory_space=pltpu.HBM)
 SM = pl.BlockSpec(memory_space=pltpu.SMEM)
 
 
-def pack_kernel(side, cond, start, label, texture, face, block, up, down, mate, away):
+def pack_kernel(
+    side, cond, start, label, texture, face, out, up, down, mate, away, block, sem
+):
     side_c = side[0]
 
     def row(x, carry):
@@ -89,6 +96,8 @@
         return carry
 
     lax.fori_loop(0, BLK, row, 0)
+    copy = pltpu.make_async_copy(block, out, sem)
+    copy.start()
     base_mate = (BLK - DEEP) * (1 - side_c)
     base_away = (BLK - DEEP) * side_c
 
@@ -110,6 +119,7 @@
         return carry
 
     lax.fori_loop(0, DEEP, ends, 0)
+    copy.wait()
 
 
 def pack(side, region_cond, start, label, texture, face):
@@ -124,7 +134,11 @@
             shape((BLK, DEEP + 2, PATS, NZ), F32),
         ),
         in_specs=[SM, SM, VM, VM, VM, VM],
-        out_specs=(VM,) * 5,
+        out_specs=(HB,) + (VM,) * 4,
+        scratch_shapes=[
+            pltpu.VMEM((BLK, BLK + 2, PATS, NZ), F32),
+            pltpu.SemaphoreType.DMA,
+        ],
         compiler_params=vmem(40),
     )(side, region_cond, start, label, texture, face)
 
@@ -200,7 +214,8 @@
 def main_kernel(
     side, marks, block, low, high, mate, away, cmate, caway,
     out_u, out_z, out_scale, out_chunk,
-    fa, fb, fc, faces, cond, cx, cy, cz, diag, scale, volt,
+    own, ub, fa, fb, fc, za, zb, faces, cond, cx, cy, cz, diag, scale, volt,
+    marked, marked_s, sem, in_sems, out_sems,
 ):
     side_c = side[0]
     lane = lax.broadcasted_iota(jnp.int32, (PATS, NZ), 1)
@@ -208,6 +223,28 @@
     last_lane = lane == NZ - 1
 
     zero = jnp.zeros((PATS, NZ), F32)
+    mid = pl.ds(DEEP, BLK)
+    above_mate = 1 - side_c
+    places = (
+        (block, BLK, mid, mid, 1),
+        (low, BLK, pl.ds(0, DEEP), mid, 1),
+        (high, BLK, pl.ds(DEEP + BLK, DEEP), mid, 1),
+        (mate, DEEP, mid, pl.ds(above_mate * (DEEP + BLK), DEEP), 2 * above_mate),
+        (away, DEEP, mid, pl.ds(side_c * (DEEP + BLK), DEEP), 2 * side_c),
+    )
+    planes, fields = [], []
+    for src, count, xs, ys, which in places:
+        rows = pl.ds(pl.multiple_of(which * BLK, BLK), BLK)
+        planes.append((src.at[:, count], cond.at[xs, rows]))
+        planes.append((src.at[:, count + 1], faces.at[xs, which]))
+        fields.append((src.at[:, pl.ds(0, count)], fa.at[xs, ys]))
+    fields.append((block.at[:, pl.ds(0, BLK)], own))
+    copies = [
+        pltpu.make_async_copy(src, dst, in_sems.at[n])
+        for n, (src, dst) in enumerate(planes + fields)
+    ]
+    for copy in copies:
+        copy.start()
 
     def clear(i, carry):
         for j in range(DEEP):
@@ -223,35 +260,7 @@
             faces[i, which] = zero
             cond[i, which * BLK : (which + 1) * BLK] = zero
 
-    def put_row(dst, src, x):
-        for j in range(BLK):
-            fa[dst, DEEP + j] = src[x, j]
-        cond[dst, BLK : 2 * BLK] = src[x, COND]
-        faces[dst, 1] = src[x, FACE]
-
-    def own_rows(x, carry):
-        put_row(DEEP + x, block, x)
-        return carry
-
-    def halo_rows(x, carry):
-        put_row(x, low, x)
-        put_row(DEEP + BLK + x, high, x)
-        return carry
-
-    lax.fori_loop(0, BLK, own_rows, 0)
-    lax.fori_loop(0, DEEP, halo_rows, 0)
-
-    def put_sides(below, above, cbelow, cabove):
-        def side_rows(x, carry):
-            for j in range(DEEP):
-                fa[DEEP + x, j] = below[x, j]
-                fa[DEEP + x, DEEP + BLK + j] = above[x, j]
-            for src, which in ((below, 0), (above, 2)):
-                cond[DEEP + x, which * BLK : (which + 1) * BLK] = src[x, DEEP]
-                faces[DEEP + x, which] = src[x, DEEP + 1]
-            return carry
-
-        lax.fori_loop(0, BLK, side_rows, 0)
+    def put_corners(cbelow, cabove):
         at = 0
         for which_x, i, k in corner_blocks():
             x = i if which_x == 0 else DEEP + BLK + i
@@ -266,11 +275,25 @@
 
     @pl.when(side_c == 0)
     def _():
-        put_sides(away, mate, caway, cmate)
+        put_corners(caway, cmate)
 
     @pl.when(side_c == 1)
     def _():
-        put_sides(mate, away, cmate, caway)
+        put_corners(cmate, caway)
+
+    for copy in copies[: len(planes)]:
+        copy.wait()
+
+    marked[...] = jnp.zeros_like(marked)
+
+    def mark_rows(x, carry):
+        for which in range(3):
+            marked[which, pl.ds(x, 1)] = faces[x, which, 0:1]
+        return carry
+
+    lax.fori_loop(0, EXT, mark_rows, 0)
+    marks_copy = pltpu.make_async_copy(marked, marked_s, sem)
+    marks_copy.start()
 
     wide_lane = lax.broadcasted_iota(jnp.int32, (ROWS, NZ), 1)
 
@@ -307,7 +330,10 @@
         )
         positive = total > 0
         diag[x] = total
-        scale[x] = jnp.where(positive, lax.rsqrt(jnp.where(positive, total, 1.0)), 0.0)
+        safe = jnp.where(positive, total, 1.0)
+        root = lax.rsqrt(safe)
+        root = root * (1.5 - 0.5 * safe * root * root)
+        scale[x] = jnp.where(positive, root, 0.0)
         return carry
 
     lax.fori_loop(0, EXT, diagonals, 0)
@@ -315,45 +341,67 @@
     def at_row(ref, x, y):
         return ref[x, pl.ds(y + YOFF, 1), :]
 
-    def neighbours(src, x, y, below, here, above):
-        weight = at_row(cz, x, y)
-        return (
-            at_row(cx, x - 1, y) * src[x - 1, y]
-            + at_row(cx, x, y) * src[x + 1, y]
-            + at_row(cy, x, y - 1) * below
-            + at_row(cy, x, y) * above
-            + weight * pltpu.roll(here, NZ - 1, 1)
-            + pltpu.roll(weight * here, 1, 1)
-        )
+    def along_z(src, x, y):
+        weight, here = at_row(cz, x, y), src[x, y]
+        return weight * pltpu.roll(here, NZ - 1, 1) + pltpu.roll(weight * here, 1, 1)
 
     def sweep(radius, src, finish):
         lo, hi = DEEP - radius, DEEP + BLK + radius
-
-        def row(x, carry):
+        for y in range(lo, hi):
+            za[y] = along_z(src, lo, y)
+
+        def row(x, ready, coming):
             below, here = src[x, lo - 1], src[x, lo]
             for y in range(lo, hi):
+                coming[y] = along_z(src, x + 1, y)
                 above = src[x, y + 1]
-                finish(x, y, here, neighbours(src, x, y, below, here, above))
+                total = (
+                    at_row(cx, x - 1, y) * src[x - 1, y]
+                    + at_row(cx, x, y) * src[x + 1, y]
+                    + at_row(cy, x, y - 1) * below
+                    + at_row(cy, x, y) * above
+                    + ready[y]
+                )
+                finish(x, y, here, total)
                 below, here = here, above
+
+        def two_rows(i, carry):
+            row(lo + 2 * i, za, zb)
+            row(lo + 2 * i + 1, zb, za)
             return carry
 
-        lax.fori_loop(lo, hi, row, 0)
+        lax.fori_loop(0, (hi - lo) // 2, two_rows, 0)
 
     def residual(x, y, here, total):
-        which, spot = (
-            (0, y + YOFF) if y < DEEP
-            else (1, y - DEEP) if y < DEEP + BLK
-            else (2, y - DEEP - BLK)
-        )
-        face = faces[x, which]
-        source = jnp.where(
-            first_lane,
-            pltpu.roll(face, (NZ - spot) % NZ, 1),
-            jnp.where(last_lane, pltpu.roll(face, NZ - 1 - UPPER - spot, 1), 0.0),
-        )
-        fb[x, y] = at_row(scale, x, y) * (source - at_row(diag, x, y) * here + total)
-
+        fb[x, y] = at_row(scale, x, y) * (total - at_row(diag, x, y) * here)
+
+    for copy in copies[len(planes) :]:
+        copy.wait()
     sweep(DEEP - 1, fa, residual)
+    marks_copy.wait()
+
+    def add_sources(x, carry):
+        for which in range(3):
+
+            @pl.when(marked_s[which, x, MARK] > 0)
+            def _():
+                face = faces[x, which]
+                start = (1, DEEP, DEEP + BLK)[which]
+                stop = (DEEP, DEEP + BLK, EXT - 1)[which]
+                for y in range(start, stop):
+                    spot = (y + YOFF, y - DEEP, y - DEEP - BLK)[which]
+                    source = jnp.where(
+                        first_lane,
+                        pltpu.roll(face, (NZ - spot) % NZ, 1),
+                        jnp.where(
+                            last_lane, pltpu.roll(face, NZ - 1 - UPPER - spot, 1), 0.0
+                        ),
+                    )
+                    fb[x, y] = fb[x, y] + at_row(scale, x, y) * source
+
+        return carry
+
+    lax.fori_loop(1, EXT - 1, add_sources, 0)
 
     def rescale(x, carry):
         here = scale[x]
@@ -385,19 +433,19 @@
     sweep(4, fa, mapped(fc))
     gram_first = gram(fa, (fb, fc), DEEP)
 
-    def save(dst, src):
-        def row(x, carry):
-            for y in range(BLK):
-                dst[x, y] = src[DEEP + x, DEEP + y]
-            return carry
-
-        lax.fori_loop(0, BLK, row, 0)
-
-    save(out_u, fa)
+    def save(x, carry):
+        for y in range(BLK):
+            ub[x, y] = fa[DEEP + x, DEEP + y]
+        return carry
+
+    lax.fori_loop(0, BLK, save, 0)
+    copy_u = pltpu.make_async_copy(ub, out_u, out_sems.at[0])
+    copy_u.start()
     smooth(1, fc, fb, fa)
+    copy_z = pltpu.make_async_copy(fb.at[mid, mid], out_z, out_sems.at[1])
+    copy_z.start()
     sweep(0, fb, mapped(fa))
     gram_second = gram(fb, (fc, fa), DEEP)
-    save(out_z, fb)
 
     def save_scale(x, carry):
         out_scale[x] = scale[DEEP + x, BLK : 2 * BLK]
@@ -423,9 +471,9 @@
                 for dy in range(PATCH):
                     x, y = x0 + dx, y0 + dy
                     weight = out_scale[x, pl.ds(y, 1), :]
-                    sums[0] += block[x, y]
-                    sums[1] += weight * out_u[x, y]
-                    sums[2] += weight * out_z[x, y]
+                    sums[0] += own[x, y]
+                    sums[1] += weight * ub[x, y]
+                    sums[2] += weight * fb[DEEP + x, DEEP + y]
             for f in range(3):
                 total = jnp.sum(jnp.where(wanted, sums[f], 0.0), axis=1, keepdims=True)
                 volt[f] = volt[f] + jnp.where(elane == mark - 1, total, 0.0)
@@ -434,20 +482,24 @@
 
     lax.fori_loop(0, 2 * half * half, electrode, 0)
 
-    grams = jnp.concatenate(
-        [gram_first, gram_second, jnp.zeros((PATS, NZ - 4 * PATS), F32)], axis=1
-    )
     per = ELECTRODES // 8
+    empty = jnp.zeros((PATS, 3 * per), F32)
+    grams = jnp.concatenate([empty, gram_first], axis=1)
+    rest = jnp.concatenate(
+        [gram_second[:8], gram_second[8:], jnp.zeros((8, NZ - 4 * PATS), F32)], axis=1
+    )
     for d in range(8):
         tile, spot = d * per // NZ, d * per % NZ
-        picked = zero
+        picked = grams
         for f in range(3):
             part = volt[f, :, tile * NZ : (tile + 1) * NZ]
             part = pltpu.roll(part, (per * f - spot) % NZ, 1)
             inside = (lane >= per * f) & (lane < per * (f + 1))
             picked = jnp.where(inside, part, picked)
         out_chunk[d, 0:PATS] = picked
-        out_chunk[d, PATS : 2 * PATS] = grams
+        out_chunk[d, PATS:] = rest
+    copy_u.wait()
+    copy_z.wait()
 
 
 def main_call(side, marks, block, low, high, mate, away, cmate, caway):
@@ -460,15 +512,24 @@
             shape((BLK, BLK, PATS, NZ), F32),
             shape((BLK, BLK, PATS, NZ), F32),
             shape((BLK, BLK, NZ), F32),
-            shape((8, 2 * PATS, NZ), F32),
+            shape((8, PATS + 8, NZ), F32),
         ),
-        in_specs=[SM, SM] + [VM] * 7,
-        out_specs=(VM,) * 4,
+        in_specs=[SM, SM] + [HB] * 5 + [VM] * 2,
+        out_specs=(HB, HB, VM, VM),
         scratch_shapes=[
+            pltpu.VMEM((BLK, BLK, PATS, NZ), F32),
+            pltpu.VMEM((BLK, BLK, PATS, NZ), F32),
             field, field, field,
+            pltpu.VMEM((EXT, PATS, NZ), F32),
+            pltpu.VMEM((EXT, PATS, NZ), F32),
             pltpu.VMEM((EXT, 3, PATS, NZ), F32),
             plane, plane, plane, plane, plane, plane,
             pltpu.VMEM((3, PATS, ELECTRODES), F32),
+            pltpu.VMEM((3, MARKROWS, NZ), F32),
+            pltpu.SMEM((3, MARKROWS, NZ), F32),
+            pltpu.SemaphoreType.DMA,
+            pltpu.SemaphoreType.DMA((16,)),
+            pltpu.SemaphoreType.DMA((2,)),
         ],
         compiler_params=vmem(60),
     )(side, marks, block, low, high, mate, away, cmate, caway)
@@ -476,16 +537,18 @@
 
 def solve_kernel(parts, out_mix, out_volt):
     volts = parts[0, 0:PATS]
-    grams = parts[0, PATS : 2 * PATS]
+    rest = parts[0, PATS:]
     for i in range(1, parts.shape[0]):
         volts = volts + parts[i, 0:PATS]
-        grams = grams + parts[i, PATS : 2 * PATS]
+        rest = rest + parts[i, PATS:]
     lane = lax.broadcasted_iota(jnp.int32, (PATS, NZ), 1)
-
-    a_at, b_at, c_at, e_at = 0, PATS, 2 * PATS, 3 * PATS
+    second = jnp.concatenate([rest, pltpu.roll(rest, NZ - 2 * PATS, 1)], axis=0)
+
+    a_at, b_at = (volts, NZ - 2 * PATS), (volts, NZ - PATS)
+    c_at, e_at = (second, 0), (second, PATS)
 
     def move(source, target):
-        return pltpu.roll(grams, (target - source) % NZ, 1)
+        return pltpu.roll(source[0], (target - source[1]) % NZ, 1)
 
     def pick(first, second, third):
         return jnp.where(
@@ -531,7 +594,26 @@
     )(parts)
 
 
-def update_kernel(mix, start, u, z, scale, out):
+PARTS = 4
+
+
+def update_kernel(
+    mix, scale, start_h, u_h, z_h, out_h, start, u, z, out, in_sems, out_sems
+):
+    count = BLK // PARTS
+    reads, writes = [], []
+    for n in range(PARTS):
+        xs = pl.ds(n * count, count)
+        pairs = ((u_h.at[xs], u.at[xs]), (z_h.at[xs], z.at[xs]), (start_h.at[:, xs], start.at[:, xs]))
+        reads.append(
+            [
+                pltpu.make_async_copy(src, dst, in_sems.at[3 * n + m])
+                for m, (src, dst) in enumerate(pairs)
+            ]
+        )
+        writes.append(pltpu.make_async_copy(out.at[:, xs], out_h.at[:, xs], out_sems.at[n]))
+        for copy in reads[n]:
+            copy.start()
     left = jnp.concatenate(
         [jnp.concatenate([part] * 3, axis=1) for part in split3(mix[...])], axis=0
     )
@@ -539,8 +621,8 @@
     def row(x, carry):
         data = jnp.concatenate(
             [
-                jnp.concatenate([u[x, y] for y in range(BLK)], axis=1),
-                jnp.concatenate([z[x, y] for y in range(BLK)], axis=1),
+                jnp.concatenate([field[x, y] for y in range(BLK)], axis=1)
+                for field in (u, z)
             ],
             axis=0,
         )
@@ -557,17 +639,30 @@
         out[:, x] = start[:, x] + pltpu.einshape("ypz->pyz", change)
         return carry
 
-    lax.fori_loop(0, BLK, row, 0)
+    for n in range(PARTS):
+        for copy in reads[n]:
+            copy.wait()
+        lax.fori_loop(n * count, (n + 1) * count, row, 0)
+        writes[n].start()
+    for copy in writes:
+        copy.wait()
 
 
 def update(mix, start, u, z, scale):
+    block = pltpu.VMEM((BLK, BLK, PATS, NZ), F32)
     return pl.pallas_call(
         update_kernel,
         out_shape=jax.ShapeDtypeStruct(start.shape, F32),
-        in_specs=[VM] * 5,
-        out_specs=VM,
-        compiler_params=vmem(24),
-    )(mix, start, u, z, scale)
+        in_specs=[VM, VM, HB, HB, HB],
+        out_specs=HB,
+        scratch_shapes=[
+            pltpu.VMEM((PATS, BLK, BLK, NZ), F32), block, block,
+            pltpu.VMEM((PATS, BLK, BLK, NZ), F32),
+            pltpu.SemaphoreType.DMA((3 * PARTS,)),
+            pltpu.SemaphoreType.DMA((PARTS,)),
+        ],
+        compiler_params=vmem(60),
+    )(mix, scale, start, u, z)
 
 
 def face_blocks(electrode_map, currents, contact_gain):
@@ -576,9 +671,11 @@
     contact = jnp.einsum("fxye,e->xyf", onehot, contact_gain, precision=HIGHEST)
     source = jnp.einsum("fxye,ep->fxpy", onehot, currents, precision=HIGHEST)
     gap = lambda width: jnp.zeros((BLK, PATS, width), F32)
+    marked = (jnp.max(electrode_map, axis=(0, 2)) > 0).astype(F32)
+    marked = jnp.broadcast_to(marked[:, None, None], (BLK, PATS, 1))
     return jnp.concatenate(
         [
-            source[0], gap(CONTACT - BLK), contact, gap(UPPER - CONTACT - 2),
+            source[0], gap(CONTACT - BLK), contact, marked, gap(UPPER - MARK - 1),
             source[1], gap(NZ - UPPER - BLK),
         ],
         axis=2,
@@ -586,8 +683,8 @@
 
 
 def body(start_field, currents, electrode_map, contact_gain, region_label, region_cond, texture):
-    gx, gy = lax.axis_size("gx"), lax.axis_size("gy")
-    side = (lax.axis_index("gy") % 2).astype(jnp.int32).reshape(1)
+    gx, gy = lax.axis_size(GX), lax.axis_size(GY)
+    side = lax.axis_index("c").astype(jnp.int32).reshape(1)
     marks = electrode_map[:, ::PATCH, ::PATCH].reshape(-1)
     face = face_blocks(electrode_map, currents, contact_gain)
     block, up, down, mate, away = pack(
@@ -599,23 +696,26 @@
     gaps = [(i, i + 1) for i in range(1, gy - 1, 2)]
     within = pairs + [(j, i) for i, j in pairs]
     across = gaps + [(j, i) for i, j in gaps]
-    low = lax.ppermute(up, "gx", rise)
-    high = lax.ppermute(down, "gx", fall)
-    away = lax.ppermute(away, "gy", across)
-    mate = lax.ppermute(mate, "gy", within)
+    low = lax.ppermute(up, GX, rise)
+    high = lax.ppermute(down, GX, fall)
+    away = lax.ppermute(away, GY, across)
+    mate = lax.ppermute(mate, GY, within)
     cmate, caway = corners(side, low, high)
-    caway = lax.ppermute(caway, "gy", across)
-    cmate = lax.ppermute(cmate, "gy", within)
+    caway = lax.ppermute(caway, GY, across)
+    cmate = lax.ppermute(cmate, GY, within)
     u, z, scale, chunk = main_call(
         side, marks, block, low, high, mate, away, cmate, caway
     )
-    chunk = lax.all_to_all(chunk, "gy", 0, 0, tiled=True)
-    chunk = jnp.sum(chunk, axis=0)
-    parts = jnp.broadcast_to(chunk[None], (gx,) + chunk.shape)
-    parts = lax.all_to_all(parts, "gx", 0, 0, tiled=True)
+    nx, nz = lax.axis_size("x"), lax.axis_size("z")
+    parts = jnp.broadcast_to(chunk[None], (nx,) + chunk.shape)
+    parts = parts.reshape((nx * gy,) + chunk.shape[1:])
+    parts = lax.all_to_all(parts, ("x", "y", "c"), 0, 0, tiled=True)
+    chunk = jnp.sum(parts, axis=0)
+    parts = jnp.broadcast_to(chunk[None], (nz,) + chunk.shape)
+    parts = lax.all_to_all(parts, "z", 0, 0, tiled=True)
     mix, volt = solve_small(parts)
     volts = jnp.broadcast_to(volt[None], (gy,) + volt.shape)
-    volts = lax.all_to_all(volts, "gy", 0, 0, tiled=True)
+    volts = lax.all_to_all(volts, GY, 0, 0, tiled=True)
     result = update(mix, start_field, u, z, scale)
     per = ELECTRODES // gy
     voltages = volts[:, :, :per].transpose(1, 0, 2).reshape(PATS, ELECTRODES)
@@ -623,19 +723,20 @@
 
 
 def solution(mesh):
+    torus = Mesh(mesh.devices.reshape(8, 4, 4, 2), GX + GY)
     placed = (
-        P(None, "gx", "gy", None),
+        P(None, GX, GY, None),
         P(),
-        P(None, "gx", "gy"),
+        P(None, GX, GY),
         P(),
-        P("gx", "gy", None),
+        P(GX, GY, None),
         P(),
-        P("gx", "gy", None),
+        P(GX, GY, None),
     )
     return jax.shard_map(
         body,
-        mesh=mesh,
+        mesh=torus,
         in_specs=placed,
-        out_specs=(P(None, "gx", "gy", None), P()),
+        out_specs=(P(None, GX, GY, None), P()),
         check_vma=False,
     )

time: 190 us -> 174 us (0.916)
  Pallas kernels: 80.3 us -> 70.1 us
  blocking collectives: 38.3 us -> 35.4 us
  local copies, waits for them, and re-layouts: 8.33 us -> 5.68 us
  starting transfers between devices: 21.1 us -> 19.2 us
    pallas_call x1, Pallas kernels: 67.7 us -> 55.7 us  [main_call(): pl.pallas_call(main_kernel, out_shape=(shape((BLK, BLK, PATS, NZ), F32),...]
    unnamed x24 -> x20, local copies, waits for them, and re-layouts: 5.72 us -> 2.08 us
    all_to_all x2, blocking collectives: 38.3 us -> 35.4 us  [the longest x1 19.7 us: body(): parts = lax.all_to_all(parts, ('x', 'y', 'c'), 0, 0, tiled=True)]
    all_to_all x1, starting transfers between devices: 6.54 us -> 4.63 us  [body(): volts = lax.all_to_all(volts, GY, 0, 0, tiled=True)]
  transfers between devices with their start and end apart: 7 -> 7, of which waited for: 3 -> 3; matrix products, arithmetic and copies ran while one was open for 0% -> 0% of each run, Pallas kernels for 3% -> 5%
where the time goes in v2:
time: 174 us; the launch traced here: 172 us
  Pallas kernels  70.1 us (40%)
  waiting for transfers between devices  36.4 us (21%)
  blocking collectives  35.4 us (20%)
  starting transfers between devices  19.2 us (11%)
  local copies, waits for them, and re-layouts  5.68 us (3%)
  matrix products  3.62 us (2%)
    pallas_call x1, Pallas kernels, main_call(): pl.pallas_call(main_kernel, out_shape=(shape((BLK, BLK, PATS, NZ), F32),...  55.7 us
    ppermute x1, waiting for transfers between devices, body(): low = lax.ppermute(up, GX, rise)  22.2 us
    all_to_all x1, blocking collectives, body(): parts = lax.all_to_all(parts, ('x', 'y', 'c'), 0, 0, tiled=True)  19.7 us
    all_to_all x1, blocking collectives, body(): parts = lax.all_to_all(parts, 'z', 0, 0, tiled=True)  15.7 us
    ppermute x1, waiting for transfers between devices, body(): caway = lax.ppermute(caway, GY, across)  10.3 us
    pallas_call x1, Pallas kernels, update(): pl.pallas_call(update_kernel, out_shape=jax.ShapeDtypeStruct(start.shape,...  6.82 us
    all_to_all x1, starting transfers between devices, body(): volts = lax.all_to_all(volts, GY, 0, 0, tiled=True)  4.63 us
    ppermute x1, starting transfers between devices, body(): low = lax.ppermute(up, GX, rise)  4.15 us
  transfers between devices with their start and end apart: 7, of which 3 were waited for; matrix products, arithmetic and copies ran while one was open for 0% of the time, Pallas kernels for 5%

profile of v2, /device:TPU:1, one launch (start us, length us, event | category | flops | bytes accessed | tf_op | source)
XLA Modules:
  0.0 172.2 jit_solution(16682087399104060879)
XLA Ops:
  0.6 0.0 copy-start
  0.6 0.0 copy-start.1
  0.7 1.0 reduce_max.9
  1.7 1.8 %fusion = f32[1,2,16,16]{3,0,2,1:T(1,128)S(1)} fusion(f32[256,1,1,1]{0,1,3,2:T(1,128)} %bitcast.24, s32[256]{0:T(256)S(1)} %iota_add_fusion, s32[2,16,16]{2,1,0:T(8,128)} %param.9), kind=kOutput, calls=%fused_computation.1 | convolution fusion | flops 1703936 | bytes 6144 | tf_op jit(solution)/shard_map/fxye,e->xyf/dot_general | solution.py:671
  3.5 0.2 copy.13
  3.7 1.8 %convolution_bitcast_fusion = f32[2,16,16,16]{3,2,1,0:T(8,128)S(1)} fusion(s32[256]{0:T(256)S(1)} %iota_add_fusion, s32[2,16,16]{2,1,0:T(8,128)} %param.9, f32[256,16]{0,1:T(8,128)S(1)} %copy-done), kind=kOutput, calls=%fused_computation | convolution fusion | flops 25296896 | bytes 52224 | tf_op jit(solution)/shard_map/fxye,ep->fxpy/dot_general | solution.py:672
  5.5 0.1 broadcast_in_dim.15
  5.7 0.3 concatenate.3.face
  6.0 3.3 %shard_map.86 = (f32[16,18,16,128]{3,2,1,0:T(8,128)S(1)}, f32[9,18,16,128]{3,2,1,0:T(8,128)S(1)}, f32[9,18,16,128]{3,2,1,0:T(8,128)S(1)}, f32[16,11,16,128]{3,2,1,0:T(8,128)}, f32[16,11,16,128]{3,2,1,0:T(8,128)}) custom-call(s32[1]{0:T(128)} %bitcast.side, f32[8]{0:T(128)S(1)} %copy-done.8, f32[16,16,16,128]{3,2,1,0:T(8,128)S(1)} %copy-done.1, ...), custom_call_target="tpu_custom_call" | custom-call | tf_op jit(solution)/shard_map/pallas_call | solution.py:127
  9.3 1.4 copy-done.4
  10.8 4.1 %collective-permute-start = (f32[9,18,16,128]{3,2,1,0:T(8,128)S(1)}, f32[9,18,16,128]{3,2,1,0:T(8,128)S(1)}, u32[]{:S(2)}, u32[]{:S(2)}) collective-permute-start(f32[9,18,16,128]{3,2,1,0:T(8,128)S(1)} %get-tuple-element.16), channel_id=1, source_target_pairs={{0,8},{8,16},{16,24},{24,32},{32,40},{40,48},{48,56},{56,64},{64,7... | collective-permute-start | bytes 3981320 | tf_op jit(solution)/shard_map/ppermute | solution.py:699
  14.9 1.3 collective-permute-start.1
  16.2 1.0 collective-permute-start.2
  17.3 3.1 %collective-permute-start.3 = (f32[16,11,16,128]{3,2,1,0:T(8,128)}, f32[16,11,16,128]{3,2,1,0:T(8,128)}, u32[]{:S(2)}, u32[]{:S(2)}) collective-permute-start(f32[16,11,16,128]{3,2,1,0:T(8,128)} %get-tuple-element.19), channel_id=1, source_target_pairs={{1,2},{3,4},{5,6},{2,1},{4,3},{6,5},{9,10},{11,12},{13,14},{10,9},... | collective-permute-start | bytes 4325384 | tf_op jit(solution)/shard_map/ppermute | solution.py:701
  20.4 22.2 %collective-permute-done.low = f32[9,18,16,128]{3,2,1,0:T(8,128)S(1)} collective-permute-done((f32[9,18,16,128]{3,2,1,0:T(8,128)S(1)}, f32[9,18,16,128]{3,2,1,0:T(8,128)S(1)}, u32[]{:S(2)}, u32[]{:S(2)}) %collective-permute-start) | collective-permute-done | bytes 1327136 | tf_op jit(solution)/shard_map/ppermute | solution.py:699
  42.6 3.9 %collective-permute-done.1.high = f32[9,18,16,128]{3,2,1,0:T(8,128)S(1)} collective-permute-done((f32[9,18,16,128]{3,2,1,0:T(8,128)S(1)}, f32[9,18,16,128]{3,2,1,0:T(8,128)S(1)}, u32[]{:S(2)}, u32[]{:S(2)}) %collective-permute-start.1) | collective-permute-done | bytes 1327136 | tf_op jit(solution)/shard_map/ppermute | solution.py:700
  46.5 1.1 shard_map.87
  47.6 1.9 %collective-permute-start.4 = (f32[104,16,128]{2,1,0:T(8,128)}, f32[104,16,128]{2,1,0:T(8,128)}, u32[]{:S(2)}, u32[]{:S(2)}) collective-permute-start(f32[104,16,128]{2,1,0:T(8,128)} %get-tuple-element.20), channel_id=1, source_target_pairs={{0,1},{2,3},{4,5},{6,7},{1,0},{3,2},{5,4},{7,6},{8,9},{10,11},{12,... | collective-permute-start | bytes 2555912 | tf_op jit(solution)/shard_map/ppermute | solution.py:705
  49.5 3.1 %collective-permute-start.5 = (f32[104,16,128]{2,1,0:T(8,128)S(1)}, f32[104,16,128]{2,1,0:T(8,128)}, u32[]{:S(2)}, u32[]{:S(2)}) collective-permute-start(f32[104,16,128]{2,1,0:T(8,128)S(1)} %get-tuple-element.21), channel_id=1, source_target_pairs={{1,2},{3,4},{5,6},{2,1},{4,3},{6,5},{9,10},{11,12},{13,14},{10,9},... | collective-permute-start | bytes 2555912 | tf_op jit(solution)/shard_map/ppermute | solution.py:704
  52.6 0.1 slice.12
  52.7 0.6 reshape.31.marks
  53.3 10.3 %collective-permute-done.5.caway = f32[104,16,128]{2,1,0:T(8,128)} collective-permute-done((f32[104,16,128]{2,1,0:T(8,128)S(1)}, f32[104,16,128]{2,1,0:T(8,128)}, u32[]{:S(2)}, u32[]{:S(2)}) %collective-permute-start.5) | collective-permute-done | bytes 852000 | tf_op jit(solution)/shard_map/ppermute | solution.py:704
  63.6 55.7 %shard_map.88 = (f32[16,16,16,128]{3,2,1,0:T(8,128)}, f32[16,16,16,128]{3,2,1,0:T(8,128)}, f32[16,16,128]{2,1,0:T(8,128)}, f32[8,24,128]{2,1,0:T(8,128)}) custom-call(s32[1]{0:T(128)} %bitcast.side, s32[128]{0:T(128)} %reshape.31.marks, f32[16,18,16,128]{3,2,1,0:T(8,128)} %copy-done.4, f32[9,18,16,128]{3,2,1,0:T(8,128)} %copy-done.2, ...), custom_call_target="tpu_custom_call" | custom-call | tf_op jit(solution)/shard_map/pallas_call | solution.py:509
  119.3 0.9 broadcast_in_dim.18
  120.2 19.7 %all_to_all.15 = f32[32,24,128]{2,1,0:T(8,128)S(1)} all-to-all(f32[32,24,128]{2,1,0:T(8,128)S(1)} %bitcast.22), channel_id=1, replica_groups=mesh['z'=8,'x'=4,'y'=4,'c'=2] {'x','y','c'}, dimensions={0} | all-to-all | bytes 786432 | tf_op jit(solution)/shard_map/all_to_all | solution.py:712
  140.0 15.7 %all_to_all.16.parts = f32[8,24,128]{2,1,0:T(8,128)S(1)} all-to-all(f32[8,24,128]{2,1,0:T(8,128)S(1)} %broadcast_in_dim.19), channel_id=1, replica_groups=mesh['z'=8,'x'=4,'y'=4,'c'=2] {'z'}, dimensions={0} | all-to-all | bytes 196608 | tf_op jit(solution)/shard_map/all_to_all | solution.py:715
  155.7 3.1 %shard_map.89 = (f32[16,32]{1,0:T(8,128)S(1)}, f32[16,128]{1,0:T(8,128)S(1)}) custom-call(f32[8,24,128]{2,1,0:T(8,128)S(1)} %all_to_all.16.parts), custom_call_target="tpu_custom_call" | custom-call | tf_op jit(solution)/shard_map/pallas_call | solution.py:588
  158.8 0.6 copy-done.7
  159.4 0.6 broadcast_in_dim.20
  160.0 4.6 %all-to-all-start.2 = ((f32[8,16,128]{2,1,0:T(8,128)}), f32[8,16,128]{2,1,0:T(8,128)S(1)}, u32[]{:S(2)}, u32[]{:S(2)}) async-start(f32[8,16,128]{2,1,0:T(8,128)} %broadcast_in_dim.20), calls=%async_computation.2 | async-start | bytes 131072 | tf_op jit(solution)/shard_map/all_to_all | solution.py:718
  164.6 6.8 %shard_map.90 = f32[16,16,16,128]{3,2,1,0:T(8,128)} custom-call(f32[16,32]{1,0:T(8,128)} %copy-done.7, f32[16,16,128]{2,1,0:T(8,128)} %get-tuple-element.24.scale, f32[16,16,16,128]{3,2,1,0:T(8,128)} %start_h.1, f32[16,16,16,128]{3,2,1,0:T(8,128)} %get-tuple-element.25.u_h, f32[16,16,16,128]{3,2,1,0:T(8,128)} %get-tuple-element.26.z_h), custom_call_target="tpu_custom_call" | custom-call | tf_op jit(solution)/shard_map/pallas_call | solution.py:653
  171.5 0.7 reshape.33
  (30 shorter events, 0.2 us)
Async XLA Ops:
  0.6 3.1 %copy-start = (f32[256,16]{0,1:T(8,128)S(1)}, f32[256,16]{0,1:T(8,128)}, u32[]{:S(2)}) copy-start(f32[256,16]{0,1:T(8,128)} %param.8) | copy-start | bytes 49156
  0.6 5.3 %copy-start.1 = (f32[16,16,16,128]{3,2,1,0:T(8,128)S(1)}, f32[16,16,16,128]{3,2,1,0:T(8,128)}, u32[]{:S(2)}) copy-start(f32[16,16,16,128]{3,2,1,0:T(8,128)} %start_h.1) | copy-start | bytes 6291460
  0.7 5.3 %copy-start.6 = (f32[16,16,128]{2,1,0:T(8,128)S(1)}, f32[16,16,128]{2,1,0:T(8,128)}, u32[]{:S(2)}) copy-start(f32[16,16,128]{2,1,0:T(8,128)} %texture.1) | copy-start | bytes 393220
  0.7 5.3 %copy-start.8 = (f32[8]{0:T(128)S(1)}, f32[8]{0:T(128)}, u32[]{:S(2)}) copy-start(f32[8]{0:T(128)} %cond.1) | copy-start | bytes 100
  0.7 5.3 %copy-start.5 = (s32[16,16,128]{2,1,0:T(8,128)S(1)}, s32[16,16,128]{2,1,0:T(8,128)}, u32[]{:S(2)}) copy-start(s32[16,16,128]{2,1,0:T(8,128)} %label.1) | copy-start | bytes 393220
  9.3 1.4 copy-start.4
  10.8 41.8 %copy-start.9 = (s32[2,16,16]{2,1,0:T(8,128)S(1)}, s32[2,16,16]{2,1,0:T(8,128)}, u32[]{:S(2)}) copy-start(s32[2,16,16]{2,1,0:T(8,128)} %param.9) | copy-start | bytes 6148
  10.8 31.9 %collective-permute-start = (f32[9,18,16,128]{3,2,1,0:T(8,128)S(1)}, f32[9,18,16,128]{3,2,1,0:T(8,128)S(1)}, u32[]{:S(2)}, u32[]{:S(2)}) collective-permute-start(f32[9,18,16,128]{3,2,1,0:T(8,128)S(1)} %get-tuple-element.16), channel_id=1, source_target_pairs={{0,8},{8,16},{16,24},{24,32},{32,40},{40,48},{48,56},{56,64},{64,7... | collective-permute-start | bytes 3981320 | tf_op jit(solution)/shard_map/ppermute | solution.py:699
  14.9 31.6 %collective-permute-start.1 = (f32[9,18,16,128]{3,2,1,0:T(8,128)S(1)}, f32[9,18,16,128]{3,2,1,0:T(8,128)S(1)}, u32[]{:S(2)}, u32[]{:S(2)}) collective-permute-start(f32[9,18,16,128]{3,2,1,0:T(8,128)S(1)} %get-tuple-element.17), channel_id=1, source_target_pairs={{8,0},{16,8},{24,16},{32,24},{40,32},{48,40},{56,48},{64,56},{72,6... | collective-permute-start | bytes 3981320 | tf_op jit(solution)/shard_map/ppermute | solution.py:700
  16.2 37.1 %collective-permute-start.2 = (f32[16,11,16,128]{3,2,1,0:T(8,128)}, f32[16,11,16,128]{3,2,1,0:T(8,128)}, u32[]{:S(2)}, u32[]{:S(2)}) collective-permute-start(f32[16,11,16,128]{3,2,1,0:T(8,128)} %get-tuple-element.18), channel_id=1, source_target_pairs={{0,1},{2,3},{4,5},{6,7},{1,0},{3,2},{5,4},{7,6},{8,9},{10,11},{12,... | collective-permute-start | bytes 4325384 | tf_op jit(solution)/shard_map/ppermute | solution.py:702
  17.3 36.1 %collective-permute-start.3 = (f32[16,11,16,128]{3,2,1,0:T(8,128)}, f32[16,11,16,128]{3,2,1,0:T(8,128)}, u32[]{:S(2)}, u32[]{:S(2)}) collective-permute-start(f32[16,11,16,128]{3,2,1,0:T(8,128)} %get-tuple-element.19), channel_id=1, source_target_pairs={{1,2},{3,4},{5,6},{2,1},{4,3},{6,5},{9,10},{11,12},{13,14},{10,9},... | collective-permute-start | bytes 4325384 | tf_op jit(solution)/shard_map/ppermute | solution.py:701
  42.6 21.0 %copy-start.2 = (f32[9,18,16,128]{3,2,1,0:T(8,128)}, f32[9,18,16,128]{3,2,1,0:T(8,128)S(1)}, u32[]{:S(2)}) copy-start(f32[9,18,16,128]{3,2,1,0:T(8,128)S(1)} %collective-permute-done.low) | copy-start | bytes 3981316
  46.5 17.1 %copy-start.3 = (f32[9,18,16,128]{3,2,1,0:T(8,128)}, f32[9,18,16,128]{3,2,1,0:T(8,128)S(1)}, u32[]{:S(2)}) copy-start(f32[9,18,16,128]{3,2,1,0:T(8,128)S(1)} %collective-permute-done.1.high) | copy-start | bytes 3981316
  47.6 5.7 %collective-permute-start.4 = (f32[104,16,128]{2,1,0:T(8,128)}, f32[104,16,128]{2,1,0:T(8,128)}, u32[]{:S(2)}, u32[]{:S(2)}) collective-permute-start(f32[104,16,128]{2,1,0:T(8,128)} %get-tuple-element.20), channel_id=1, source_target_pairs={{0,1},{2,3},{4,5},{6,7},{1,0},{3,2},{5,4},{7,6},{8,9},{10,11},{12,... | collective-permute-start | bytes 2555912 | tf_op jit(solution)/shard_map/ppermute | solution.py:705
  49.5 14.1 %collective-permute-start.5 = (f32[104,16,128]{2,1,0:T(8,128)S(1)}, f32[104,16,128]{2,1,0:T(8,128)}, u32[]{:S(2)}, u32[]{:S(2)}) collective-permute-start(f32[104,16,128]{2,1,0:T(8,128)S(1)} %get-tuple-element.21), channel_id=1, source_target_pairs={{1,2},{3,4},{5,6},{2,1},{4,3},{6,5},{9,10},{11,12},{13,14},{10,9},... | collective-permute-start | bytes 2555912 | tf_op jit(solution)/shard_map/ppermute | solution.py:704
  158.8 0.6 copy-start.7
  160.0 11.5 %all-to-all-start.2 = ((f32[8,16,128]{2,1,0:T(8,128)}), f32[8,16,128]{2,1,0:T(8,128)S(1)}, u32[]{:S(2)}, u32[]{:S(2)}) async-start(f32[8,16,128]{2,1,0:T(8,128)} %broadcast_in_dim.20), calls=%async_computation.2 | async-start | bytes 131072 | tf_op jit(solution)/shard_map/all_to_all | solution.py:718

commit v3 on v2

--- a/solution.py
+++ b/solution.py
@@ -28,7 +28,6 @@
 FACE = BLK + 1
 UPPER = 64
 CONTACT = 32
-MARK = 34
 MARKROWS = 40
 
 F32 = jnp.float32
@@ -243,7 +242,7 @@
         pltpu.make_async_copy(src, dst, in_sems.at[n])
         for n, (src, dst) in enumerate(planes + fields)
     ]
-    for copy in copies:
+    for copy in copies[:-1]:
         copy.start()
 
     def clear(i, carry):
@@ -288,7 +287,7 @@
 
     def mark_rows(x, carry):
         for which in range(3):
-            marked[which, pl.ds(x, 1)] = faces[x, which, 0:1]
+            marked[which, pl.ds(x, 1)] = jnp.sum(faces[x, which], axis=0, keepdims=True)
         return carry
 
     lax.fori_loop(0, EXT, mark_rows, 0)
@@ -375,15 +374,17 @@
     def residual(x, y, here, total):
         fb[x, y] = at_row(scale, x, y) * (total - at_row(diag, x, y) * here)
 
-    for copy in copies[len(planes) :]:
+    for copy in copies[len(planes) : -1]:
         copy.wait()
+    copies[-1].start()
     sweep(DEEP - 1, fa, residual)
     marks_copy.wait()
+    copies[-1].wait()
 
     def add_sources(x, carry):
         for which in range(3):
 
-            @pl.when(marked_s[which, x, MARK] > 0)
+            @pl.when(marked_s[which, x, CONTACT] + marked_s[which, x, CONTACT + 1] > 0)
             def _():
                 face = faces[x, which]
                 start = (1, DEEP, DEEP + BLK)[which]
@@ -496,8 +497,9 @@
             part = pltpu.roll(part, (per * f - spot) % NZ, 1)
             inside = (lane >= per * f) & (lane < per * (f + 1))
             picked = jnp.where(inside, part, picked)
-        out_chunk[d, 0:PATS] = picked
-        out_chunk[d, PATS:] = rest
+        for copy in range(out_chunk.shape[0]):
+            out_chunk[copy, d, 0:PATS] = picked
+            out_chunk[copy, d, PATS:] = rest
     copy_u.wait()
     copy_z.wait()
 
@@ -512,7 +514,7 @@
             shape((BLK, BLK, PATS, NZ), F32),
             shape((BLK, BLK, PATS, NZ), F32),
             shape((BLK, BLK, NZ), F32),
-            shape((8, PATS + 8, NZ), F32),
+            shape((4, 8, PATS + 8, NZ), F32),
         ),
         in_specs=[SM, SM] + [HB] * 5 + [VM] * 2,
         out_specs=(HB, HB, VM, VM),
@@ -671,11 +673,9 @@
     contact = jnp.einsum("fxye,e->xyf", onehot, contact_gain, precision=HIGHEST)
     source = jnp.einsum("fxye,ep->fxpy", onehot, currents, precision=HIGHEST)
     gap = lambda width: jnp.zeros((BLK, PATS, width), F32)
-    marked = (jnp.max(electrode_map, axis=(0, 2)) > 0).astype(F32)
-    marked = jnp.broadcast_to(marked[:, None, None], (BLK, PATS, 1))
     return jnp.concatenate(
         [
-            source[0], gap(CONTACT - BLK), contact, marked, gap(UPPER - MARK - 1),
+            source[0], gap(CONTACT - BLK), contact, gap(UPPER - CONTACT - 2),
             source[1], gap(NZ - UPPER - BLK),
         ],
         axis=2,
@@ -706,9 +706,8 @@
     u, z, scale, chunk = main_call(
         side, marks, block, low, high, mate, away, cmate, caway
     )
-    nx, nz = lax.axis_size("x"), lax.axis_size("z")
-    parts = jnp.broadcast_to(chunk[None], (nx,) + chunk.shape)
-    parts = parts.reshape((nx * gy,) + chunk.shape[1:])
+    nz = lax.axis_size("z")
+    parts = chunk.reshape((-1,) + chunk.shape[2:])
     parts = lax.all_to_all(parts, ("x", "y", "c"), 0, 0, tiled=True)
     chunk = jnp.sum(parts, axis=0)
     parts = jnp.broadcast_to(chunk[None], (nz,) + chunk.shape)

time: 174 us -> 172 us (0.989); the launches traced: 172 us -> 172 us
  no operation moved by 1% of the time
where the time goes in v3:
time: 172 us
  Pallas kernels  71.2 us (41%)
  waiting for transfers between devices  36.4 us (21%)
  blocking collectives  36 us (21%)
  starting transfers between devices  19.2 us (11%)
  local copies, waits for them, and re-layouts  4.66 us (3%)
  matrix products  3.77 us (2%)
    pallas_call x1, Pallas kernels, main_call(): pl.pallas_call(main_kernel, out_shape=(shape((BLK, BLK, PATS, NZ), F32),...  56.9 us
    ppermute x1, waiting for transfers between devices, body(): low = lax.ppermute(up, GX, rise)  22.2 us
    all_to_all x1, blocking collectives, body(): parts = lax.all_to_all(parts, ('x', 'y', 'c'), 0, 0, tiled=True)  20.2 us
    all_to_all x1, blocking collectives, body(): parts = lax.all_to_all(parts, 'z', 0, 0, tiled=True)  15.8 us
    ppermute x1, waiting for transfers between devices, body(): caway = lax.ppermute(caway, GY, across)  10.2 us
    pallas_call x1, Pallas kernels, update(): pl.pallas_call(update_kernel, out_shape=jax.ShapeDtypeStruct(start.shape,...  6.82 us
    all_to_all x1, starting transfers between devices, body(): volts = lax.all_to_all(volts, GY, 0, 0, tiled=True)  4.63 us
    ppermute x1, starting transfers between devices, body(): low = lax.ppermute(up, GX, rise)  4.15 us
  transfers between devices with their start and end apart: 7, of which 3 were waited for; matrix products, arithmetic and copies ran while one was open for 0% of the time, Pallas kernels for 5%

profile of v3, /device:TPU:1, one launch (start us, length us, event | category | flops | bytes accessed | tf_op | source)
XLA Modules:
  0.0 172.1 jit_solution(768874889687363714)
XLA Ops:
  0.6 0.0 copy-start
  0.6 0.0 copy-start.1
  0.7 1.9 %fusion = f32[1,2,16,16]{3,0,2,1:T(1,128)S(1)} fusion(f32[256,1,1,1]{0,1,3,2:T(1,128)} %bitcast.24, s32[256]{0:T(256)S(1)} %iota_add_fusion, s32[2,16,16]{2,1,0:T(8,128)} %param.9), kind=kOutput, calls=%fused_computation.1 | convolution fusion | flops 1703936 | bytes 6144 | tf_op jit(solution)/shard_map/fxye,e->xyf/dot_general | solution.py:673
  2.7 0.2 copy.12
  2.8 1.8 %convolution_bitcast_fusion = f32[2,16,16,16]{3,2,1,0:T(8,128)S(1)} fusion(s32[256]{0:T(256)S(1)} %iota_add_fusion, s32[2,16,16]{2,1,0:T(8,128)} %param.9, f32[256,16]{0,1:T(8,128)S(1)} %copy-done), kind=kOutput, calls=%fused_computation | convolution fusion | flops 25296896 | bytes 52224 | tf_op jit(solution)/shard_map/fxye,ep->fxpy/dot_general | solution.py:674
  4.8 0.2 concatenate.3.face
  5.0 3.3 %shard_map.86 = (f32[16,18,16,128]{3,2,1,0:T(8,128)S(1)}, f32[9,18,16,128]{3,2,1,0:T(8,128)S(1)}, f32[9,18,16,128]{3,2,1,0:T(8,128)S(1)}, f32[16,11,16,128]{3,2,1,0:T(8,128)}, f32[16,11,16,128]{3,2,1,0:T(8,128)}) custom-call(s32[1]{0:T(128)} %bitcast.side, f32[8]{0:T(128)S(1)} %copy-done.8, f32[16,16,16,128]{3,2,1,0:T(8,128)S(1)} %copy-done.1, ...), custom_call_target="tpu_custom_call" | custom-call | tf_op jit(solution)/shard_map/pallas_call | solution.py:126
  8.4 1.4 copy-done.4
  9.8 4.1 %collective-permute-start = (f32[9,18,16,128]{3,2,1,0:T(8,128)S(1)}, f32[9,18,16,128]{3,2,1,0:T(8,128)S(1)}, u32[]{:S(2)}, u32[]{:S(2)}) collective-permute-start(f32[9,18,16,128]{3,2,1,0:T(8,128)S(1)} %get-tuple-element.16), channel_id=1, source_target_pairs={{0,8},{8,16},{16,24},{24,32},{32,40},{40,48},{48,56},{56,64},{64,7... | collective-permute-start | bytes 3981320 | tf_op jit(solution)/shard_map/ppermute | solution.py:699
  13.9 1.3 collective-permute-start.1
  15.2 1.0 collective-permute-start.2
  16.3 3.1 %collective-permute-start.3 = (f32[16,11,16,128]{3,2,1,0:T(8,128)}, f32[16,11,16,128]{3,2,1,0:T(8,128)}, u32[]{:S(2)}, u32[]{:S(2)}) collective-permute-start(f32[16,11,16,128]{3,2,1,0:T(8,128)} %get-tuple-element.19), channel_id=1, source_target_pairs={{1,2},{3,4},{5,6},{2,1},{4,3},{6,5},{9,10},{11,12},{13,14},{10,9},... | collective-permute-start | bytes 4325384 | tf_op jit(solution)/shard_map/ppermute | solution.py:701
  19.4 22.2 %collective-permute-done.low = f32[9,18,16,128]{3,2,1,0:T(8,128)S(1)} collective-permute-done((f32[9,18,16,128]{3,2,1,0:T(8,128)S(1)}, f32[9,18,16,128]{3,2,1,0:T(8,128)S(1)}, u32[]{:S(2)}, u32[]{:S(2)}) %collective-permute-start) | collective-permute-done | bytes 1327136 | tf_op jit(solution)/shard_map/ppermute | solution.py:699
  41.6 3.9 %collective-permute-done.1.high = f32[9,18,16,128]{3,2,1,0:T(8,128)S(1)} collective-permute-done((f32[9,18,16,128]{3,2,1,0:T(8,128)S(1)}, f32[9,18,16,128]{3,2,1,0:T(8,128)S(1)}, u32[]{:S(2)}, u32[]{:S(2)}) %collective-permute-start.1) | collective-permute-done | bytes 1327136 | tf_op jit(solution)/shard_map/ppermute | solution.py:700
  45.5 1.1 shard_map.87
  46.7 1.9 %collective-permute-start.4 = (f32[104,16,128]{2,1,0:T(8,128)}, f32[104,16,128]{2,1,0:T(8,128)}, u32[]{:S(2)}, u32[]{:S(2)}) collective-permute-start(f32[104,16,128]{2,1,0:T(8,128)} %get-tuple-element.20), channel_id=1, source_target_pairs={{0,1},{2,3},{4,5},{6,7},{1,0},{3,2},{5,4},{7,6},{8,9},{10,11},{12,... | collective-permute-start | bytes 2555912 | tf_op jit(solution)/shard_map/ppermute | solution.py:705
  48.5 3.1 %collective-permute-start.5 = (f32[104,16,128]{2,1,0:T(8,128)S(1)}, f32[104,16,128]{2,1,0:T(8,128)}, u32[]{:S(2)}, u32[]{:S(2)}) collective-permute-start(f32[104,16,128]{2,1,0:T(8,128)S(1)} %get-tuple-element.21), channel_id=1, source_target_pairs={{1,2},{3,4},{5,6},{2,1},{4,3},{6,5},{9,10},{11,12},{13,14},{10,9},... | collective-permute-start | bytes 2555912 | tf_op jit(solution)/shard_map/ppermute | solution.py:704
  51.6 0.1 slice.12
  51.7 0.7 reshape.24.marks
  52.4 0.0 collective-permute-done.2.mate
  52.4 0.0 collective-permute-done.3.away
  52.4 0.0 collective-permute-done.4.cmate
  52.4 10.2 %collective-permute-done.5.caway = f32[104,16,128]{2,1,0:T(8,128)} collective-permute-done((f32[104,16,128]{2,1,0:T(8,128)S(1)}, f32[104,16,128]{2,1,0:T(8,128)}, u32[]{:S(2)}, u32[]{:S(2)}) %collective-permute-start.5) | collective-permute-done | bytes 852000 | tf_op jit(solution)/shard_map/ppermute | solution.py:704
  62.6 56.9 %shard_map.88 = (f32[16,16,16,128]{3,2,1,0:T(8,128)}, f32[16,16,16,128]{3,2,1,0:T(8,128)}, f32[16,16,128]{2,1,0:T(8,128)}, f32[4,8,24,128]{3,2,1,0:T(8,128)}) custom-call(s32[1]{0:T(128)} %bitcast.side, s32[128]{0:T(128)} %reshape.24.marks, f32[16,18,16,128]{3,2,1,0:T(8,128)} %copy-done.4, f32[9,18,16,128]{3,2,1,0:T(8,128)} %copy-done.2, ...), custom_call_target="tpu_custom_call" | custom-call | tf_op jit(solution)/shard_map/pallas_call | solution.py:511
  119.5 20.2 %all_to_all.15 = f32[32,24,128]{2,1,0:T(8,128)S(1)} all-to-all(f32[32,24,128]{2,1,0:T(8,128)} %bitcast.23), channel_id=1, replica_groups=mesh['z'=8,'x'=4,'y'=4,'c'=2] {'x','y','c'}, dimensions={0} | all-to-all | bytes 786432 | tf_op jit(solution)/shard_map/all_to_all | solution.py:711
  139.7 15.8 %all_to_all.16.parts = f32[8,24,128]{2,1,0:T(8,128)S(1)} all-to-all(f32[8,24,128]{2,1,0:T(8,128)S(1)} %broadcast_in_dim.26), channel_id=1, replica_groups=mesh['z'=8,'x'=4,'y'=4,'c'=2] {'z'}, dimensions={0} | all-to-all | bytes 196608 | tf_op jit(solution)/shard_map/all_to_all | solution.py:714
  155.5 3.1 %shard_map.89 = (f32[16,32]{1,0:T(8,128)S(1)}, f32[16,128]{1,0:T(8,128)S(1)}) custom-call(f32[8,24,128]{2,1,0:T(8,128)S(1)} %all_to_all.16.parts), custom_call_target="tpu_custom_call" | custom-call | tf_op jit(solution)/shard_map/pallas_call | solution.py:590
  158.6 0.6 copy-done.7
  159.2 0.6 broadcast_in_dim.27
  159.9 4.6 %all-to-all-start.2 = ((f32[8,16,128]{2,1,0:T(8,128)}), f32[8,16,128]{2,1,0:T(8,128)S(1)}, u32[]{:S(2)}, u32[]{:S(2)}) async-start(f32[8,16,128]{2,1,0:T(8,128)} %broadcast_in_dim.27), calls=%async_computation.2 | async-start | bytes 131072 | tf_op jit(solution)/shard_map/all_to_all | solution.py:717
  164.5 6.8 %shard_map.90 = f32[16,16,16,128]{3,2,1,0:T(8,128)} custom-call(f32[16,32]{1,0:T(8,128)} %copy-done.7, f32[16,16,128]{2,1,0:T(8,128)} %get-tuple-element.24.scale, f32[16,16,16,128]{3,2,1,0:T(8,128)} %start_h.1, f32[16,16,16,128]{3,2,1,0:T(8,128)} %get-tuple-element.25.u_h, f32[16,16,16,128]{3,2,1,0:T(8,128)} %get-tuple-element.26.z_h), custom_call_target="tpu_custom_call" | custom-call | tf_op jit(solution)/shard_map/pallas_call | solution.py:655
  171.4 0.7 reshape.26
  (26 shorter events, 0.2 us)
Async XLA Ops:
  0.6 2.2 %copy-start = (f32[256,16]{0,1:T(8,128)S(1)}, f32[256,16]{0,1:T(8,128)}, u32[]{:S(2)}) copy-start(f32[256,16]{0,1:T(8,128)} %param.8) | copy-start | bytes 49156
  0.6 4.4 %copy-start.1 = (f32[16,16,16,128]{3,2,1,0:T(8,128)S(1)}, f32[16,16,16,128]{3,2,1,0:T(8,128)}, u32[]{:S(2)}) copy-start(f32[16,16,16,128]{3,2,1,0:T(8,128)} %start_h.1) | copy-start | bytes 6291460
  0.7 4.4 %copy-start.6 = (f32[16,16,128]{2,1,0:T(8,128)S(1)}, f32[16,16,128]{2,1,0:T(8,128)}, u32[]{:S(2)}) copy-start(f32[16,16,128]{2,1,0:T(8,128)} %texture.1) | copy-start | bytes 393220
  0.7 4.4 %copy-start.8 = (f32[8]{0:T(128)S(1)}, f32[8]{0:T(128)}, u32[]{:S(2)}) copy-start(f32[8]{0:T(128)} %cond.1) | copy-start | bytes 100
  0.7 4.4 %copy-start.5 = (s32[16,16,128]{2,1,0:T(8,128)S(1)}, s32[16,16,128]{2,1,0:T(8,128)}, u32[]{:S(2)}) copy-start(s32[16,16,128]{2,1,0:T(8,128)} %label.1) | copy-start | bytes 393220
  8.4 1.4 copy-start.4
  9.8 41.8 %copy-start.9 = (s32[2,16,16]{2,1,0:T(8,128)S(1)}, s32[2,16,16]{2,1,0:T(8,128)}, u32[]{:S(2)}) copy-start(s32[2,16,16]{2,1,0:T(8,128)} %param.9) | copy-start | bytes 6148
  9.8 31.9 %collective-permute-start = (f32[9,18,16,128]{3,2,1,0:T(8,128)S(1)}, f32[9,18,16,128]{3,2,1,0:T(8,128)S(1)}, u32[]{:S(2)}, u32[]{:S(2)}) collective-permute-start(f32[9,18,16,128]{3,2,1,0:T(8,128)S(1)} %get-tuple-element.16), channel_id=1, source_target_pairs={{0,8},{8,16},{16,24},{24,32},{32,40},{40,48},{48,56},{56,64},{64,7... | collective-permute-start | bytes 3981320 | tf_op jit(solution)/shard_map/ppermute | solution.py:699
  13.9 31.6 %collective-permute-start.1 = (f32[9,18,16,128]{3,2,1,0:T(8,128)S(1)}, f32[9,18,16,128]{3,2,1,0:T(8,128)S(1)}, u32[]{:S(2)}, u32[]{:S(2)}) collective-permute-start(f32[9,18,16,128]{3,2,1,0:T(8,128)S(1)} %get-tuple-element.17), channel_id=1, source_target_pairs={{8,0},{16,8},{24,16},{32,24},{40,32},{48,40},{56,48},{64,56},{72,6... | collective-permute-start | bytes 3981320 | tf_op jit(solution)/shard_map/ppermute | solution.py:700
  15.2 37.1 %collective-permute-start.2 = (f32[16,11,16,128]{3,2,1,0:T(8,128)}, f32[16,11,16,128]{3,2,1,0:T(8,128)}, u32[]{:S(2)}, u32[]{:S(2)}) collective-permute-start(f32[16,11,16,128]{3,2,1,0:T(8,128)} %get-tuple-element.18), channel_id=1, source_target_pairs={{0,1},{2,3},{4,5},{6,7},{1,0},{3,2},{5,4},{7,6},{8,9},{10,11},{12,... | collective-permute-start | bytes 4325384 | tf_op jit(solution)/shard_map/ppermute | solution.py:702
  16.3 36.1 %collective-permute-start.3 = (f32[16,11,16,128]{3,2,1,0:T(8,128)}, f32[16,11,16,128]{3,2,1,0:T(8,128)}, u32[]{:S(2)}, u32[]{:S(2)}) collective-permute-start(f32[16,11,16,128]{3,2,1,0:T(8,128)} %get-tuple-element.19), channel_id=1, source_target_pairs={{1,2},{3,4},{5,6},{2,1},{4,3},{6,5},{9,10},{11,12},{13,14},{10,9},... | collective-permute-start | bytes 4325384 | tf_op jit(solution)/shard_map/ppermute | solution.py:701
  41.6 21.0 %copy-start.2 = (f32[9,18,16,128]{3,2,1,0:T(8,128)}, f32[9,18,16,128]{3,2,1,0:T(8,128)S(1)}, u32[]{:S(2)}) copy-start(f32[9,18,16,128]{3,2,1,0:T(8,128)S(1)} %collective-permute-done.low) | copy-start | bytes 3981316
  45.5 17.1 %copy-start.3 = (f32[9,18,16,128]{3,2,1,0:T(8,128)}, f32[9,18,16,128]{3,2,1,0:T(8,128)S(1)}, u32[]{:S(2)}) copy-start(f32[9,18,16,128]{3,2,1,0:T(8,128)S(1)} %collective-permute-done.1.high) | copy-start | bytes 3981316
  46.7 5.7 %collective-permute-start.4 = (f32[104,16,128]{2,1,0:T(8,128)}, f32[104,16,128]{2,1,0:T(8,128)}, u32[]{:S(2)}, u32[]{:S(2)}) collective-permute-start(f32[104,16,128]{2,1,0:T(8,128)} %get-tuple-element.20), channel_id=1, source_target_pairs={{0,1},{2,3},{4,5},{6,7},{1,0},{3,2},{5,4},{7,6},{8,9},{10,11},{12,... | collective-permute-start | bytes 2555912 | tf_op jit(solution)/shard_map/ppermute | solution.py:705
  48.5 14.1 %collective-permute-start.5 = (f32[104,16,128]{2,1,0:T(8,128)S(1)}, f32[104,16,128]{2,1,0:T(8,128)}, u32[]{:S(2)}, u32[]{:S(2)}) collective-permute-start(f32[104,16,128]{2,1,0:T(8,128)S(1)} %get-tuple-element.21), channel_id=1, source_target_pairs={{1,2},{3,4},{5,6},{2,1},{4,3},{6,5},{9,10},{11,12},{13,14},{10,9},... | collective-permute-start | bytes 2555912 | tf_op jit(solution)/shard_map/ppermute | solution.py:704
  158.6 0.6 copy-start.7
  159.9 11.5 %all-to-all-start.2 = ((f32[8,16,128]{2,1,0:T(8,128)}), f32[8,16,128]{2,1,0:T(8,128)S(1)}, u32[]{:S(2)}, u32[]{:S(2)}) async-start(f32[8,16,128]{2,1,0:T(8,128)} %broadcast_in_dim.27), calls=%async_computation.2 | async-start | bytes 131072 | tf_op jit(solution)/shard_map/all_to_all | solution.py:717

commit v4 on v3

--- a/solution.py
+++ b/solution.py
@@ -138,7 +138,7 @@
             pltpu.VMEM((BLK, BLK + 2, PATS, NZ), F32),
             pltpu.SemaphoreType.DMA,
         ],
-        compiler_params=vmem(40),
+        compiler_params=vmem(57),
     )(side, region_cond, start, label, texture, face)
 
 
@@ -592,7 +592,7 @@
         out_shape=(shape((PATS, 2 * PATS), F32), shape((PATS, NZ), F32)),
         in_specs=[VM],
         out_specs=(VM, VM),
-        compiler_params=vmem(16),
+        compiler_params=vmem(60),
     )(parts)
 
 

time: 172 us -> 176 us (1.023)
  Pallas kernels: 71.2 us -> 75.1 us
    pallas_call x1, Pallas kernels: 3.32 us -> 6.14 us  [pack(): pl.pallas_call(pack_kernel, out_shape=(shape((BLK, BLK + 2, PATS, NZ), F3...]
    unnamed x20 -> x8, local copies, waits for them, and re-layouts: 2.07 us -> 0.02 us
where the time goes in v4:
time: 176 us; the launch traced here: 175 us
  Pallas kernels  75.1 us (43%)
  waiting for transfers between devices  36.6 us (21%)
  blocking collectives  35.6 us (20%)
  starting transfers between devices  19 us (11%)
  local copies, waits for them, and re-layouts  3.96 us (2%)
  matrix products  3.62 us (2%)
    pallas_call x1, Pallas kernels, main_call(): pl.pallas_call(main_kernel, out_shape=(shape((BLK, BLK, PATS, NZ), F32),...  56.4 us
    ppermute x1, waiting for transfers between devices, body(): low = lax.ppermute(up, GX, rise)  22.6 us
    all_to_all x1, blocking collectives, body(): parts = lax.all_to_all(parts, ('x', 'y', 'c'), 0, 0, tiled=True)  20.5 us
    all_to_all x1, blocking collectives, body(): parts = lax.all_to_all(parts, 'z', 0, 0, tiled=True)  15.1 us
    ppermute x1, waiting for transfers between devices, body(): caway = lax.ppermute(caway, GY, across)  10.2 us
    pallas_call x1, Pallas kernels, update(): pl.pallas_call(update_kernel, out_shape=jax.ShapeDtypeStruct(start.shape,...  6.82 us
    pallas_call x1, Pallas kernels, pack(): pl.pallas_call(pack_kernel, out_shape=(shape((BLK, BLK + 2, PATS, NZ), F3...  6.14 us
    all_to_all x1, starting transfers between devices, body(): volts = lax.all_to_all(volts, GY, 0, 0, tiled=True)  4.63 us
  transfers between devices with their start and end apart: 7, of which 3 were waited for; matrix products, arithmetic and copies ran while one was open for 0% of the time, Pallas kernels for 5%

profile of v4, /device:TPU:1, one launch (start us, length us, event | category | flops | bytes accessed | tf_op | source)
XLA Modules:
  0.0 174.8 jit_solution(780489347384775495)
XLA Ops:
  0.6 0.0 copy-start
  0.7 1.8 %fusion = f32[1,2,16,16]{3,0,2,1:T(1,128)S(1)} fusion(f32[256,1,1,1]{0,1,3,2:T(1,128)} %bitcast.24, s32[256]{0:T(256)S(1)} %iota_add_fusion, s32[2,16,16]{2,1,0:T(8,128)} %param.9), kind=kOutput, calls=%fused_computation.1 | convolution fusion | flops 1703936 | bytes 6144 | tf_op jit(solution)/shard_map/fxye,e->xyf/dot_general | solution.py:673
  2.5 0.2 copy.12
  2.6 0.0 copy-done
  2.7 1.8 %convolution_bitcast_fusion = f32[2,16,16,16]{3,2,1,0:T(8,128)S(1)} fusion(s32[256]{0:T(256)S(1)} %iota_add_fusion, s32[2,16,16]{2,1,0:T(8,128)} %param.9, f32[256,16]{0,1:T(8,128)S(1)} %copy-done), kind=kOutput, calls=%fused_computation | convolution fusion | flops 25296896 | bytes 52224 | tf_op jit(solution)/shard_map/fxye,ep->fxpy/dot_general | solution.py:674
  4.6 0.9 concatenate.3.face
  5.5 6.1 %shard_map.86 = (f32[16,18,16,128]{3,2,1,0:T(8,128)}, f32[9,18,16,128]{3,2,1,0:T(8,128)}, f32[9,18,16,128]{3,2,1,0:T(8,128)}, f32[16,11,16,128]{3,2,1,0:T(8,128)}, f32[16,11,16,128]{3,2,1,0:T(8,128)}) custom-call(s32[1]{0:T(128)} %bitcast.side, f32[8]{0:T(128)} %cond.1, f32[16,16,16,128]{3,2,1,0:T(8,128)} %start_h.1, s32[16,16,128]{2,1,0:T(8,128)} %label.1, ...), custom_call_target="tpu_custom_call" | custom-call | tf_op jit(solution)/shard_map/pallas_call | solution.py:126
  11.6 0.0 copy-start.3
  11.6 4.0 %collective-permute-start = (f32[9,18,16,128]{3,2,1,0:T(8,128)}, f32[9,18,16,128]{3,2,1,0:T(8,128)S(1)}, u32[]{:S(2)}, u32[]{:S(2)}) collective-permute-start(f32[9,18,16,128]{3,2,1,0:T(8,128)} %get-tuple-element.16), channel_id=1, source_target_pairs={{0,8},{8,16},{16,24},{24,32},{32,40},{40,48},{48,56},{56,64},{64,7... | collective-permute-start | bytes 3981320 | tf_op jit(solution)/shard_map/ppermute | solution.py:699
  15.7 1.3 collective-permute-start.1
  17.0 1.0 collective-permute-start.2
  18.0 3.1 %collective-permute-start.3 = (f32[16,11,16,128]{3,2,1,0:T(8,128)}, f32[16,11,16,128]{3,2,1,0:T(8,128)}, u32[]{:S(2)}, u32[]{:S(2)}) collective-permute-start(f32[16,11,16,128]{3,2,1,0:T(8,128)} %get-tuple-element.19), channel_id=1, source_target_pairs={{1,2},{3,4},{5,6},{2,1},{4,3},{6,5},{9,10},{11,12},{13,14},{10,9},... | collective-permute-start | bytes 4325384 | tf_op jit(solution)/shard_map/ppermute | solution.py:701
  21.1 22.6 %collective-permute-done.low = f32[9,18,16,128]{3,2,1,0:T(8,128)S(1)} collective-permute-done((f32[9,18,16,128]{3,2,1,0:T(8,128)}, f32[9,18,16,128]{3,2,1,0:T(8,128)S(1)}, u32[]{:S(2)}, u32[]{:S(2)}) %collective-permute-start) | collective-permute-done | bytes 1327136 | tf_op jit(solution)/shard_map/ppermute | solution.py:699
  43.7 3.8 %collective-permute-done.1.high = f32[9,18,16,128]{3,2,1,0:T(8,128)S(1)} collective-permute-done((f32[9,18,16,128]{3,2,1,0:T(8,128)}, f32[9,18,16,128]{3,2,1,0:T(8,128)S(1)}, u32[]{:S(2)}, u32[]{:S(2)}) %collective-permute-start.1) | collective-permute-done | bytes 1327136 | tf_op jit(solution)/shard_map/ppermute | solution.py:700
  47.4 1.2 shard_map.87
  48.6 1.9 %collective-permute-start.4 = (f32[104,16,128]{2,1,0:T(8,128)}, f32[104,16,128]{2,1,0:T(8,128)}, u32[]{:S(2)}, u32[]{:S(2)}) collective-permute-start(f32[104,16,128]{2,1,0:T(8,128)} %get-tuple-element.20), channel_id=1, source_target_pairs={{0,1},{2,3},{4,5},{6,7},{1,0},{3,2},{5,4},{7,6},{8,9},{10,11},{12,... | collective-permute-start | bytes 2555912 | tf_op jit(solution)/shard_map/ppermute | solution.py:705
  50.5 3.1 %collective-permute-start.5 = (f32[104,16,128]{2,1,0:T(8,128)S(1)}, f32[104,16,128]{2,1,0:T(8,128)}, u32[]{:S(2)}, u32[]{:S(2)}) collective-permute-start(f32[104,16,128]{2,1,0:T(8,128)S(1)} %get-tuple-element.21), channel_id=1, source_target_pairs={{1,2},{3,4},{5,6},{2,1},{4,3},{6,5},{9,10},{11,12},{13,14},{10,9},... | collective-permute-start | bytes 2555912 | tf_op jit(solution)/shard_map/ppermute | solution.py:704
  53.6 0.1 slice.12
  53.6 0.7 reshape.24.marks
  54.3 0.0 collective-permute-done.2.mate
  54.3 0.0 collective-permute-done.3.away
  54.3 0.0 collective-permute-done.4.cmate
  54.3 10.2 %collective-permute-done.5.caway = f32[104,16,128]{2,1,0:T(8,128)} collective-permute-done((f32[104,16,128]{2,1,0:T(8,128)S(1)}, f32[104,16,128]{2,1,0:T(8,128)}, u32[]{:S(2)}, u32[]{:S(2)}) %collective-permute-start.5) | collective-permute-done | bytes 852000 | tf_op jit(solution)/shard_map/ppermute | solution.py:704
  64.6 56.4 %shard_map.88 = (f32[16,16,16,128]{3,2,1,0:T(8,128)}, f32[16,16,16,128]{3,2,1,0:T(8,128)}, f32[16,16,128]{2,1,0:T(8,128)}, f32[4,8,24,128]{3,2,1,0:T(8,128)}) custom-call(s32[1]{0:T(128)} %bitcast.side, s32[128]{0:T(128)} %reshape.24.marks, f32[16,18,16,128]{3,2,1,0:T(8,128)} %get-tuple-element.15.block, f32[9,18,16,128]{3,2,1,0:T(8,128)} %copy-done.1, ...), custom_call_target="tpu_custom_call" | custom-call | tf_op jit(solution)/shard_map/pallas_call | solution.py:511
  121.0 20.5 %all_to_all.15 = f32[32,24,128]{2,1,0:T(8,128)S(1)} all-to-all(f32[32,24,128]{2,1,0:T(8,128)} %bitcast.23), channel_id=1, replica_groups=mesh['z'=8,'x'=4,'y'=4,'c'=2] {'x','y','c'}, dimensions={0} | all-to-all | bytes 786432 | tf_op jit(solution)/shard_map/all_to_all | solution.py:711
  141.6 15.1 %all_to_all.16.parts = f32[8,24,128]{2,1,0:T(8,128)} all-to-all(f32[8,24,128]{2,1,0:T(8,128)S(1)} %broadcast_in_dim.26), channel_id=1, replica_groups=mesh['z'=8,'x'=4,'y'=4,'c'=2] {'z'}, dimensions={0} | all-to-all | bytes 196608 | tf_op jit(solution)/shard_map/all_to_all | solution.py:714
  156.7 4.6 %shard_map.89 = (f32[16,32]{1,0:T(8,128)}, f32[16,128]{1,0:T(8,128)}) custom-call(f32[8,24,128]{2,1,0:T(8,128)} %all_to_all.16.parts), custom_call_target="tpu_custom_call" | custom-call | tf_op jit(solution)/shard_map/pallas_call | solution.py:590
  161.3 1.3 broadcast_in_dim.27
  162.6 4.6 %all-to-all-start.2 = ((f32[8,16,128]{2,1,0:T(8,128)}), f32[8,16,128]{2,1,0:T(8,128)S(1)}, u32[]{:S(2)}, u32[]{:S(2)}) async-start(f32[8,16,128]{2,1,0:T(8,128)} %broadcast_in_dim.27), calls=%async_computation.2 | async-start | bytes 131072 | tf_op jit(solution)/shard_map/all_to_all | solution.py:717
  167.2 6.8 %shard_map.90 = f32[16,16,16,128]{3,2,1,0:T(8,128)} custom-call(f32[16,32]{1,0:T(8,128)} %get-tuple-element.23.mix, f32[16,16,128]{2,1,0:T(8,128)} %get-tuple-element.24.scale, f32[16,16,16,128]{3,2,1,0:T(8,128)} %start_h.1, f32[16,16,16,128]{3,2,1,0:T(8,128)} %get-tuple-element.25.u_h, f32[16,16,16,128]{3,2,1,0:T(8,128)} %get-tuple-element.26.z_h), custom_call_target="tpu_custom_call" | custom-call | tf_op jit(solution)/shard_map/pallas_call | solution.py:655
  174.1 0.0 all-to-all-done.2
  174.1 0.7 reshape.26
  (14 shorter events, 0.1 us)
Async XLA Ops:
  0.6 2.0 %copy-start = (f32[256,16]{0,1:T(8,128)S(1)}, f32[256,16]{0,1:T(8,128)}, u32[]{:S(2)}) copy-start(f32[256,16]{0,1:T(8,128)} %param.8) | copy-start | bytes 49156
  11.6 41.9 %copy-start.3 = (s32[2,16,16]{2,1,0:T(8,128)S(1)}, s32[2,16,16]{2,1,0:T(8,128)}, u32[]{:S(2)}) copy-start(s32[2,16,16]{2,1,0:T(8,128)} %param.9) | copy-start | bytes 6148
  11.6 32.0 %collective-permute-start = (f32[9,18,16,128]{3,2,1,0:T(8,128)}, f32[9,18,16,128]{3,2,1,0:T(8,128)S(1)}, u32[]{:S(2)}, u32[]{:S(2)}) collective-permute-start(f32[9,18,16,128]{3,2,1,0:T(8,128)} %get-tuple-element.16), channel_id=1, source_target_pairs={{0,8},{8,16},{16,24},{24,32},{32,40},{40,48},{48,56},{56,64},{64,7... | collective-permute-start | bytes 3981320 | tf_op jit(solution)/shard_map/ppermute | solution.py:699
  15.7 31.8 %collective-permute-start.1 = (f32[9,18,16,128]{3,2,1,0:T(8,128)}, f32[9,18,16,128]{3,2,1,0:T(8,128)S(1)}, u32[]{:S(2)}, u32[]{:S(2)}) collective-permute-start(f32[9,18,16,128]{3,2,1,0:T(8,128)} %get-tuple-element.17), channel_id=1, source_target_pairs={{8,0},{16,8},{24,16},{32,24},{40,32},{48,40},{56,48},{64,56},{72,6... | collective-permute-start | bytes 3981320 | tf_op jit(solution)/shard_map/ppermute | solution.py:700
  17.0 37.4 %collective-permute-start.2 = (f32[16,11,16,128]{3,2,1,0:T(8,128)}, f32[16,11,16,128]{3,2,1,0:T(8,128)}, u32[]{:S(2)}, u32[]{:S(2)}) collective-permute-start(f32[16,11,16,128]{3,2,1,0:T(8,128)} %get-tuple-element.18), channel_id=1, source_target_pairs={{0,1},{2,3},{4,5},{6,7},{1,0},{3,2},{5,4},{7,6},{8,9},{10,11},{12,... | collective-permute-start | bytes 4325384 | tf_op jit(solution)/shard_map/ppermute | solution.py:702
  18.0 36.3 %collective-permute-start.3 = (f32[16,11,16,128]{3,2,1,0:T(8,128)}, f32[16,11,16,128]{3,2,1,0:T(8,128)}, u32[]{:S(2)}, u32[]{:S(2)}) collective-permute-start(f32[16,11,16,128]{3,2,1,0:T(8,128)} %get-tuple-element.19), channel_id=1, source_target_pairs={{1,2},{3,4},{5,6},{2,1},{4,3},{6,5},{9,10},{11,12},{13,14},{10,9},... | collective-permute-start | bytes 4325384 | tf_op jit(solution)/shard_map/ppermute | solution.py:701
  43.7 20.9 %copy-start.1 = (f32[9,18,16,128]{3,2,1,0:T(8,128)}, f32[9,18,16,128]{3,2,1,0:T(8,128)S(1)}, u32[]{:S(2)}) copy-start(f32[9,18,16,128]{3,2,1,0:T(8,128)S(1)} %collective-permute-done.low) | copy-start | bytes 3981316
  47.4 17.1 %copy-start.2 = (f32[9,18,16,128]{3,2,1,0:T(8,128)}, f32[9,18,16,128]{3,2,1,0:T(8,128)S(1)}, u32[]{:S(2)}) copy-start(f32[9,18,16,128]{3,2,1,0:T(8,128)S(1)} %collective-permute-done.1.high) | copy-start | bytes 3981316
  48.6 5.7 %collective-permute-start.4 = (f32[104,16,128]{2,1,0:T(8,128)}, f32[104,16,128]{2,1,0:T(8,128)}, u32[]{:S(2)}, u32[]{:S(2)}) collective-permute-start(f32[104,16,128]{2,1,0:T(8,128)} %get-tuple-element.20), channel_id=1, source_target_pairs={{0,1},{2,3},{4,5},{6,7},{1,0},{3,2},{5,4},{7,6},{8,9},{10,11},{12,... | collective-permute-start | bytes 2555912 | tf_op jit(solution)/shard_map/ppermute | solution.py:705
  50.5 14.1 %collective-permute-start.5 = (f32[104,16,128]{2,1,0:T(8,128)S(1)}, f32[104,16,128]{2,1,0:T(8,128)}, u32[]{:S(2)}, u32[]{:S(2)}) collective-permute-start(f32[104,16,128]{2,1,0:T(8,128)S(1)} %get-tuple-element.21), channel_id=1, source_target_pairs={{1,2},{3,4},{5,6},{2,1},{4,3},{6,5},{9,10},{11,12},{13,14},{10,9},... | collective-permute-start | bytes 2555912 | tf_op jit(solution)/shard_map/ppermute | solution.py:704
  162.6 11.5 %all-to-all-start.2 = ((f32[8,16,128]{2,1,0:T(8,128)}), f32[8,16,128]{2,1,0:T(8,128)S(1)}, u32[]{:S(2)}, u32[]{:S(2)}) async-start(f32[8,16,128]{2,1,0:T(8,128)} %broadcast_in_dim.27), calls=%async_computation.2 | async-start | bytes 131072 | tf_op jit(solution)/shard_map/all_to_all | solution.py:717
